TPU v7x, 128 devices: a whole 4x4x4 slice. The times are simulated.
128 devices in a mesh: fx: 8 (over y, x_lo), fy: 16 (over x_hi, z, core).
Axes of the slice: x: 4 (x_hi: 2, x_lo: 2; x = x_hi * 2 + x_lo), y: 4, z: 4, core: 2. Of those that a mesh axis runs over, the one named last changes fastest.
Arguments:
- sky: bfloat16 [8192, 65536], P('fx', 'fy'), may hold values from -6 to 6
- sub_off: int32 [2, 4], replicated, may hold values from 0 to 65535
- readers: int32 [128], replicated, may hold values from 0 to 3, as said below
- vis_cells: int32 [2, 262144], P(None, ('fx', 'fy')), may hold values from 0 to 504
- row_kernel: bfloat16 [8, 262144], P(None, ('fx', 'fy')), may hold values from 0.049804688 to 1
- col_kernel: float32 [8, 262144], P(None, ('fx', 'fy')), may hold values from 0.05 to 1
Outputs:
- vis: float32 [2, 262144], P(None, ('fx', 'fy'))
Inputs may be any that keep to these rules, and one draw needn't show every extreme that they name: `readers`: every subgrid is read by at least one reader.
All inputs are finite; a program needn't handle non-finite values.
Results may differ from a plain program's by a relative error of at most 0.0064.
Values may be sent and summed in bfloat16 or wider, within the bound.
A program may use at most 128 MiB of HBM per device.

v0:
```python
import math

import jax
import jax.numpy as jnp
from jax import lax
from jax.sharding import PartitionSpec as P

FACET = 4096
SUB = 512
K = 128
FX_DEV = 2
FR = 512
NSUB = 4


def phase_mod(upper, lower, sky_cells):
    return (upper % 256 * lower + upper // 256 * lower % sky_cells * 256) % sky_cells


def unit_angle(phase, sky_cells):
    return phase.astype(jnp.float32) * (2.0 * math.pi / sky_cells)


def resample_table(start, sky_cells):
    tap_index = jnp.arange(K, dtype=jnp.int32)
    grid_cells = jnp.arange(SUB, dtype=jnp.int32)
    places = (start + tap_index * (sky_cells // SUB)) % sky_cells
    forward = unit_angle(phase_mod(grid_cells[:, None], places[None, :], sky_cells), sky_cells)
    backward = -unit_angle(
        phase_mod(SUB // K * tap_index[None, :], places[:, None], sky_cells), sky_cells
    )
    wave_real, wave_imag = (jnp.cos(forward), jnp.sin(forward))
    back_real, back_imag = (jnp.cos(backward) / K, jnp.sin(backward) / K)
    highest = lax.Precision.HIGHEST
    real_part = jnp.dot(wave_real, back_real, precision=highest) - jnp.dot(
        wave_imag, back_imag, precision=highest
    )
    imag_part = jnp.dot(wave_real, back_imag, precision=highest) + jnp.dot(
        wave_imag, back_real, precision=highest
    )
    return (real_part, imag_part)


def row_stack(real_part, imag_part):
    return jnp.stack(
        [jnp.stack([real_part, -imag_part], 1), jnp.stack([imag_part, real_part], 1)], 1
    ).astype(jnp.bfloat16)


def col_stack(real_part, imag_part, factor):
    return (
        jnp.stack([jnp.stack([real_part, imag_part]), jnp.stack([-imag_part, real_part])]) * factor
    )


def strip_table(col_offsets, col_start, sky_cells):
    columns = col_start + jnp.arange(FACET, dtype=jnp.int32)
    frequency = col_offsets[:, None] + SUB // K * jnp.arange(K, dtype=jnp.int32)[None, :]
    angles = -unit_angle(
        phase_mod(frequency[None, :, :], columns[:, None, None], sky_cells), sky_cells
    )
    values_table = jnp.stack([jnp.cos(angles), jnp.sin(angles)], 2) / math.sqrt(FACET)
    return values_table.reshape(FACET, NSUB * 2 * K).astype(jnp.bfloat16)


def row_transform(row_offsets, row_start, sky_cells):
    rows_here = row_start + jnp.arange(FR, dtype=jnp.int32)
    frequency = row_offsets[:, None] + SUB // K * jnp.arange(K, dtype=jnp.int32)[None, :]
    angles = -unit_angle(
        phase_mod(frequency[:, :, None], rows_here[None, None, :], sky_cells), sky_cells
    )
    wave_real = jnp.cos(angles) / math.sqrt(FR)
    wave_imag = jnp.sin(angles) / math.sqrt(FR)
    real_rows = jnp.stack([wave_real, -wave_imag], 2)
    imag_rows = jnp.stack([wave_imag, wave_real], 2)
    return jnp.stack([real_rows, imag_rows], 1).astype(jnp.bfloat16)


def degridding(subgrid, vis_cells, row_kernel, col_kernel):
    grid_cells = jnp.arange(SUB, dtype=jnp.int32)
    row_gap = grid_cells[None, :] - vis_cells[0][:, None]
    col_gap = grid_cells[None, :] - vis_cells[1][:, None]
    row_weights = jnp.zeros(row_gap.shape, jnp.float32)
    col_weights = jnp.zeros(col_gap.shape, jnp.float32)
    for tap_index in range(row_kernel.shape[0]):
        row_weights = row_weights + jnp.where(
            row_gap == tap_index, row_kernel[tap_index].astype(jnp.float32)[:, None], 0.0
        )
        col_weights = col_weights + jnp.where(
            col_gap == tap_index, col_kernel[tap_index][:, None], 0.0
        )
    spread = jnp.dot(
        row_weights.astype(jnp.bfloat16),
        subgrid.reshape(SUB, 2 * SUB),
        preferred_element_type=jnp.float32,
    )
    spread = spread.reshape(-1, 2, SUB)
    return jnp.sum(spread * col_weights[:, None, :], axis=2).T


def local(sky, sub_off, readers, vis_cells, row_kernel, col_kernel):
    rows_axis = lax.axis_size("fx")
    cols_axis = lax.axis_size("fy")
    sky_cells = FACET * cols_axis
    facet_rows = FX_DEV * rows_axis
    row_spacing = sky_cells // facet_rows
    factor = 1.0 / math.sqrt(facet_rows * cols_axis)
    row_starts = (lax.axis_index("fx") * FX_DEV + jnp.arange(FX_DEV, dtype=jnp.int32)) * row_spacing
    col_start = lax.axis_index("fy") * FACET
    strips = jnp.dot(
        sky, strip_table(sub_off[1], col_start, sky_cells), preferred_element_type=jnp.float32
    )
    strips = strips.astype(jnp.bfloat16).reshape(FX_DEV, FR, NSUB, 2, K)

    def facet_tables(row_start):
        return (
            row_transform(sub_off[0], row_start, sky_cells),
            row_stack(*resample_table(row_start, sky_cells)),
        )

    row_tables, resamplers = jax.vmap(facet_tables)(row_starts)
    blocks = jnp.einsum(
        "fsqkpr,frspl->fsqkl", row_tables, strips, preferred_element_type=jnp.float32
    ).astype(jnp.bfloat16)
    partial_rows = jnp.einsum(
        "fmdqk,fsqkl->mdsl", resamplers, blocks, preferred_element_type=jnp.float32
    )
    col_table = col_stack(*resample_table(col_start, sky_cells), factor)
    piece = lax.psum_scatter(
        jnp.einsum(
            "mcsl,cdnl->mdsn",
            partial_rows,
            col_table,
            precision=lax.Precision.HIGHEST,
            preferred_element_type=jnp.float32,
        ),
        ("fx", "fy"),
        scatter_dimension=0,
        tiled=True,
    )
    piece = piece.astype(jnp.bfloat16)
    whole = lax.all_gather(piece, ("fx", "fy"), axis=0, tiled=True)
    chosen = readers[lax.axis_index(("fx", "fy"))]
    subgrid = lax.dynamic_index_in_dim(whole, chosen, 2, keepdims=False)
    return degridding(subgrid, vis_cells, row_kernel, col_kernel)


def solution(mesh):
    return jax.shard_map(
        local,
        mesh=mesh,
        in_specs=(
            P("fx", "fy"),
            P(),
            P(),
            P(None, ("fx", "fy")),
            P(None, ("fx", "fy")),
            P(None, ("fx", "fy")),
        ),
        out_specs=P(None, ("fx", "fy")),
        check_vma=False,
    )
```

profile of v0, /device:TPU:1, one launch (start us, length us, event | category | flops | bytes accessed | tf_op | source)
XLA Modules:
  0.0 460.0 jit_solution(11211925458557984800)
XLA Ops:
  6.7 3.4 fusion.100
  10.1 4.1 fusion.102
  14.3 1.8 fusion.115
  16.0 1.8 fusion.117
  17.9 48.4 %fusion.21 = (f32[4096,4,1,128]{0,3,2,1:T(8,128)S(1)}, f32[4096,4,1,128]{0,3,2,1:T(8,128)S(1)}) fusion(s32[4,128]{1,0:T(4,128)S(1)} %get-tuple-element.42, s32[4096]{0:T(1024)S(1)} %iota_add_fusion, s32[4,128]{1,0:T(4,128)S(1)} %get-tuple-element.43), kind=kLoop, calls=%fused_computation.33 | loop fusion | flops 60817408 | bytes 16797696 | tf_op jit(solution)/shard_map/cos | solution.py:62
  66.3 1.4 fusion
  68.5 10.1 %convert_bitcast_fusion = bf16[1024,1024]{0,1:T(8,128)(2,1)} fusion(bf16[4096,1024]{0,1:T(8,128)(2,1)S(1)} %bitcast.95, bf16[1024,4096]{1,0:T(8,128)(2,1)S(1)} %bitcast.117), kind=kOutput, calls=%fused_computation.65 | convolution fusion | flops 8590983168 | bytes 18874368 | tf_op jit(solution)/shard_map/dot_general | solution.py:110
  78.6 3.3 reshape.940
  81.9 3.4 fusion.97
  85.3 3.4 fusion.77
  88.7 1.8 convolution_add_fusion.1
  90.5 1.8 fusion.76
  92.3 10.5 %negate_convert_fusion = (bf16[2,4,128,1,512]{4,2,3,1,0:T(8,128)(2,1)S(1)}, bf16[2,4,128,1,512]{4,2,3,1,0:T(8,128)(2,1)S(1)}, bf16[2,4,128,1,512]{4,2,3,1,0:T(8,128)(2,1)S(1)}) fusion(s32[4,128]{1,0:T(4,128)S(1)} %get-tuple-element.37, s32[2,512]{1,0:T(2,128)S(1)} %iota_add_fusion.1, s32[4,128]{1,0:T(4,128)S(1)} %get-tuple-element.36), kind=kLoop, calls=%fused_computation.66 | loop fusion | flops 18350080 | bytes 3153920 | tf_op jit(solution)/shard_map/convert.15
  103.1 1.3 fusion.70
  105.3 9.0 %convolution_bitcast_fusion = f32[512,2,4,512]{0,3,2,1:T(8,128)} fusion(f32[512,2,4,128,1,1]{3,0,5,4,1,2:T(8,128)S(1)} %fusion.80, f32[1,2,512,128]{3,2,1,0:T(8,128)S(1)} %get-tuple-element.10, f32[1,2,512,128]{3,2,1,0:T(8,128)S(1)} %get-tuple-element.9), kind=kOutput, calls=%fused_computation.47 | convolution fusion | flops 6442975232 | bytes 11534336 | tf_op jit(solution)/shard_map/mcsl,cdnl->mdsn/dot_general | solution.py:130
  114.3 10.3 %copy.45 = f32[512,2,4,512]{3,2,1,0:T(4,128)} copy(f32[512,2,4,512]{0,3,2,1:T(8,128)} %convolution_bitcast_fusion) | data formatting | bytes 16777216 | tf_op jit(solution)/shard_map/mcsl,cdnl->mdsn/transpose | solution.py:130
  124.7 114.4 %all-reduce.2 = bf16[512,2,4,512]{3,2,1,0:T(4,128)(2,1)} all-reduce(f32[512,2,4,512]{3,2,1,0:T(4,128)} %copy.45), channel_id=2, replica_groups=mesh['fx'=8,'fy'=16] {'fx','fy'}, use_global_device_ids=true, to_apply=%region_0.1.clone | all-reduce | flops 2097152 | bytes 12582912
  239.1 1.4 dynamic-slice_convert_fusion
  240.6 5.7 %select_add_fusion = f32[2048,512]{1,0:T(8,128)} fusion(f32[2048]{0:T(1024)S(1)} %bitcast.104, f32[2048]{0:T(1024)S(1)} %bitcast.105, f32[2048]{0:T(1024)S(1)} %bitcast.99, f32[2048]{0:T(1024)S(1)} %bitcast.100, f32[2048]{0:T(1024)S(1)} %bitcast.101, f32[2048]{0:T(1024)S(1)} %bitcast.102, f32[2048]{0:T(1024)S(1)} %bitcast.103, f32[2048]{0:T(1024)S(1)} %bitcast.98, ...), kind=kLoop, calls=%fused_computation.22 | loop fusion | flops 25165824 | bytes 4268032 | tf_op jit(solution)/shard_map/add | solution.py:89
  246.3 5.5 %copy.47 = f32[2048,512]{0,1:T(8,128)} copy(f32[2048,512]{1,0:T(8,128)} %select_add_fusion) | data formatting | bytes 8388608 | tf_op jit(solution)/shard_map/add | solution.py:89
  254.4 181.8 %all-gather.2.cloned.1.call-done = bf16[512,2,4,512]{3,2,1,0:T(4,128)(2,1)} async-done(((bf16[4,2,4,512]{3,2,1,0:T(4,128)(2,1)}), bf16[512,2,4,512]{3,2,1,0:T(4,128)(2,1)}) %all-gather.2.cloned.1.call-update) | async-done | bytes 4194320 | tf_op jit(solution)/shard_map/all_gather | solution.py:142
  436.2 4.3 constant_dynamic-slice_fusion
  440.6 2.6 copy.60
  443.2 9.5 %multiply_reduce_fusion = f32[2048,2]{0,1:T(2,128)} fusion(f32[2048,512]{0,1:T(8,128)} %copy.47, f32[2048]{0:T(1024)S(1)} %bitcast.113, f32[2048]{0:T(1024)S(1)} %bitcast.114, f32[2048]{0:T(1024)S(1)} %bitcast.108, f32[2048]{0:T(1024)S(1)} %bitcast.109, f32[2048]{0:T(1024)S(1)} %bitcast.110, f32[2048]{0:T(1024)S(1)} %bitcast.111, f32[2048]{0:T(1024)S(1)} %bitcast.112, ...), kind=kOutput, calls=%fused_computation.17 | convolution fusion | flops 2177888256 | bytes 5332992 | tf_op jit(solution)/shard_map/dot_general | solution.py:92
  (39 shorter events, 3.0 us)
Async XLA Ops:
  6.5 429.7 %all-gather.2.cloned.1.call-start = ((), (), s32[]{:S(2)}) async-start(), calls=%async_computation | async-start | bytes 4227072 | tf_op jit(solution)/shard_map/all_gather | solution.py:142
  10.1 7.7 %copy-start.3 = (s32[2,4]{1,0:T(2,128)S(1)}, s32[2,4]{1,0:T(2,128)}, u32[]{:S(2)}) copy-start(s32[2,4]{1,0:T(2,128)} %param.7) | copy-start | bytes 100
  17.9 49.8 %slice-start = ((s8[8388608]{0:T(1024)(128)(4,1)}), s8[4194304]{0:T(1024)(128)(4,1)S(1)}, s32[]{:S(2)}) async-start(s8[8388608]{0:T(1024)(128)(4,1)} %bitcast.116), calls=%async_computation.1 | async-start | bytes 8388608
  66.3 2.2 slice-start.1
  81.9 3.4 copy-start.5
  124.7 115.8 %copy-start.2 = (s32[2,2048]{1,0:T(2,128)S(1)}, s32[2,2048]{1,0:T(2,128)}, u32[]{:S(2)}) copy-start(s32[2,2048]{1,0:T(2,128)} %param.9) | copy-start | bytes 49156
  124.7 115.9 %copy-start.1 = (f32[8,2048]{1,0:T(8,128)S(1)}, f32[8,2048]{1,0:T(8,128)}, u32[]{:S(2)}) copy-start(f32[8,2048]{1,0:T(8,128)} %param.11) | copy-start | bytes 196612
  246.3 5.5 %copy-start.4 = (s32[128]{0:T(128)S(1)}, s32[128]{0:T(128)}, u32[]{:S(2)}) copy-start(s32[128]{0:T(128)} %param.8) | copy-start | bytes 1540
  246.3 8.0 %copy-start = (bf16[8,2048]{1,0:T(8,128)(2,1)S(1)}, bf16[8,2048]{1,0:T(8,128)(2,1)}, u32[]{:S(2)}) copy-start(bf16[8,2048]{1,0:T(8,128)(2,1)} %param.10) | copy-start | bytes 98308
Sparse Core Ops, SparseCore 0:
  240.6 195.5 all-gather.1
where the time goes:
time: 468 us; the launch traced here: 460 us
  waiting for transfers between devices  182 us (39%)
  blocking collectives  114 us (24%)
  other arithmetic  66.8 us (14%)
  matrix products  51.9 us (11%)
  local copies, waits for them, and re-layouts  28.9 us (6%)
  between operations  16.1 us (3%)
    all_gather x1, waiting for transfers between devices, local(): whole = lax.all_gather(piece, ('fx', 'fy'), axis=0, tiled=True)  182 us
    unnamed x1, blocking collectives  114 us
    cos x1, other arithmetic, strip_table(): jnp.cos(angles)  48.4 us
    another operation x1, other arithmetic  10.5 us
    transpose x1, local copies, waits for them, and re-layouts, local(): jnp.einsum('mcsl,cdnl->mdsn', partial_rows, col_table, precision=lax.Prec...  10.3 us
    dot_general x1, matrix products, local(): jnp.dot(sky, strip_table(sub_off[1], col_start, sky_cells), preferred_ele...  10.1 us
    dot_general x1, matrix products, degridding(): jnp.dot(row_weights.astype(jnp.bfloat16), subgrid.reshape(SUB, 2 * SUB),...  9.5 us
  transfers between devices with their start and end apart: 1, of which 1 were waited for; matrix products, arithmetic and copies ran while one was open for 3% of the time, Pallas kernels for 0%

commit v1 on v0

v1 whole, which is shorter than its diff:
```python
import functools
import math

import jax
import jax.numpy as jnp
import numpy as np
from jax import lax
from jax.experimental import pallas as pl
from jax.experimental.pallas import tpu as pltpu
from jax.sharding import PartitionSpec as P

FACET = 4096
SUB = 512
K = 128
W = 8
FR = 512
NSUB = 4
SKY = 65536
CHUNK = 512
CHUNKS = FACET // CHUNK
VTILE = 256
BF = jnp.bfloat16
F32 = jnp.float32
MESH = pl.DeviceIdType.MESH


def wave(rows, cols, period):
    turn = (np.arange(rows)[:, None] * np.arange(cols)[None, :]) % period
    angle = turn * (2.0 * math.pi / period)
    return np.cos(angle), np.sin(angle)


def small_tables():
    re, im = wave(K, K, K)
    re, im = re / K, -im / K
    cols = np.block([[re.T, im.T], [-im.T, re.T]])
    rows = np.zeros((2, 2, K, 3, 2, 64))
    for f in range(2):
        for t in range(K):
            at, cell = divmod(32 * f + t, 64)
            rows[f, 0, :, at, 0, cell] = re[t]
            rows[f, 1, :, at, 0, cell] = -im[t]
            rows[f, 0, :, at, 1, cell] = im[t]
            rows[f, 1, :, at, 1, cell] = re[t]
    qre, qim = wave(K, FR, SKY // 4)
    scale = 1.0 / math.sqrt(FR)
    return (
        jnp.asarray(cols, BF),
        jnp.asarray(rows.reshape(4 * K, 384), BF),
        jnp.asarray(qre * scale, F32),
        jnp.asarray(-qim * scale, F32),
    )


def grid_tables():
    re, im = wave(SUB, SUB, SUB)
    et = np.stack([np.concatenate([re, im], 1), np.concatenate([-im, re], 1)])
    et = et.reshape(2, 8, 64, 2 * SUB).transpose(1, 0, 2, 3).reshape(2 * SUB, 2 * SUB)
    en = np.block([[re, -im], [im, re]]) / 16.0
    return jnp.asarray(et, BF), jnp.asarray(en, BF)


def cis(phase):
    turn = phase & 0xFFFF
    quarter = (turn + 8192) >> 14
    x = (turn - (quarter << 14)).astype(F32) * (2.0 * math.pi / SKY)
    x2 = x * x
    c = 1.0 + x2 * (-0.5 + x2 * (1.0 / 24 + x2 * (-1.0 / 720 + x2 * (1.0 / 40320))))
    s = x * (1.0 + x2 * (-1.0 / 6 + x2 * (1.0 / 120 + x2 * (-1.0 / 5040 + x2 * (1.0 / 362880)))))
    odd = (quarter & 1) == 1
    cos = jnp.where(odd, s, c)
    sin = jnp.where(odd, c, s)
    cos = jnp.where(((quarter + 1) & 2) != 0, -cos, cos)
    sin = jnp.where((quarter & 2) != 0, -sin, sin)
    return cos, sin


def iota(shape, dim):
    return lax.broadcasted_iota(jnp.int32, shape, dim)


def facet_kernel(
    sky_ref, off_ref, dc_ref, dr_ref, qre_ref, qim_ref, out_ref,
    sky_v, va, vb, acc, coarse, fine, uu, sem,
):
    fx, fy = lax.axis_index("fx"), lax.axis_index("fy")

    def sky_copy(c):
        part = pl.ds(pl.multiple_of(c * CHUNK, CHUNK), CHUNK)
        return pltpu.make_async_copy(sky_ref.at[:, part], sky_v.at[:, part], sem.at[c])

    for c in range(CHUNKS):
        sky_copy(c).start()

    step, lane = iota((64, K), 0), iota((64, K), 1)
    for s in range(NSUB):
        freq = off_ref[1, s] + 4 * lane
        cos, sin = cis(freq * (64 * step + FACET * fy) + SKY // 4 * lane * fy)
        coarse[s, 0] = cos
        coarse[s, 1] = -sin
        cos, sin = cis(freq * step)
        fine[s, 0] = cos * (1.0 / 64)
        fine[s, 1] = -sin * (1.0 / 64)

    def fill(s, c, ref):
        bre, bim = fine[s, 0], fine[s, 1]
        for h in range(CHUNK // 64):
            at = pl.ds(c * (CHUNK // 64) + h, 1)
            are, aim = coarse[s, 0, at, :], coarse[s, 1, at, :]
            ref[64 * h : 64 * h + 64, 0:K] = (are * bre - aim * bim).astype(BF)
            ref[64 * h : 64 * h + 64, K : 2 * K] = (are * bim + aim * bre).astype(BF)

    def add(c, ref):
        part = pl.ds(pl.multiple_of(c * CHUNK, CHUNK), CHUNK)
        acc[...] += jnp.dot(sky_v[:, part], ref[...], preferred_element_type=F32)

    fill(0, 0, va)
    for s in range(NSUB):
        acc[...] = jnp.zeros_like(acc)

        @pl.loop(0, CHUNKS // 2)
        def _(t):
            if s == 0:
                sky_copy(2 * t).wait()
                sky_copy(2 * t + 1).wait()
            fill(s, 2 * t + 1, vb)
            add(2 * t, va)
            last = t == CHUNKS // 2 - 1
            after = jnp.where(last, min(s + 1, NSUB - 1), s)
            fill(after, jnp.where(last, 0, 2 * t + 2), va)
            add(2 * t + 1, vb)

        places = iota((1, FR), 1)
        parts = []
        for f in range(2):
            cos, sin = cis(off_ref[0, s] * (FACET * (2 * fx + f) + places))
            qre, qim = qre_ref[...], qim_ref[...]
            ure, uim = qre * cos + qim * sin, qim * cos - qre * sin
            if f == 1:
                sign = jnp.where((iota((K, 1), 0) & 1) == 1, -1.0, 1.0)
                ure, uim = ure * sign, uim * sign
            uu[0:K] = ure.astype(BF)
            uu[K : 2 * K] = uim.astype(BF)
            strips = acc[FR * f : FR * (f + 1)].astype(BF)
            mixed = jnp.dot(uu[...], strips, preferred_element_type=F32)
            bre = mixed[:K, :K] - mixed[K:, K:]
            bim = mixed[:K, K:] + mixed[K:, :K]
            block = jnp.concatenate([bre, bim], 1).astype(BF)
            image = jnp.dot(block, dc_ref[...], preferred_element_type=F32)
            parts += [image[:, :K].T.astype(BF), image[:, K:].T.astype(BF)]
        window = jnp.dot(
            jnp.concatenate(parts, 1), dr_ref[...], preferred_element_type=F32
        ).astype(BF)
        for di in range(3):
            for dj in range(4):
                out_ref[di * 4 + dj, s] = window[32 * dj : 32 * dj + 32, 128 * di : 128 * di + 128]


def facets(sky, sub_off):
    any_space = pl.BlockSpec(memory_space=pl.ANY)
    vmem = pl.BlockSpec(memory_space=pltpu.VMEM)
    return pl.pallas_call(
        facet_kernel,
        out_shape=jax.ShapeDtypeStruct((12, NSUB, 32, 128), BF),
        in_specs=[any_space, pl.BlockSpec(memory_space=pltpu.SMEM), vmem, vmem, vmem, vmem],
        out_specs=vmem,
        scratch_shapes=[
            pltpu.VMEM((2 * FR, FACET), BF),
            pltpu.VMEM((CHUNK, 2 * K), BF),
            pltpu.VMEM((CHUNK, 2 * K), BF),
            pltpu.VMEM((2 * FR, 2 * K), F32),
            pltpu.VMEM((NSUB, 2, 64, K), F32),
            pltpu.VMEM((NSUB, 2, 64, K), F32),
            pltpu.VMEM((2 * K, FR), BF),
            pltpu.SemaphoreType.DMA((CHUNKS,)),
        ],
        compiler_params=pltpu.CompilerParams(vmem_limit_bytes=40 * 2**20),
    )(sky, sub_off, *small_tables())


def exchange_kernel(
    pieces_ref, readers_ref, out_ref,
    halo, plane, outbox, fin, halo_sems, plane_sems, last_sems,
):
    fx, fy = lax.axis_index("fx"), lax.axis_index("fy")
    y, core, z = fx // 2, fy % 2, (fy // 2) % 4
    x = 2 * (fy // 8) + fx % 2
    first = core == 0

    def device(x, y, z, core):
        return (2 * y + x % 2, (x // 2) * 8 + 2 * z + core)

    def axis_of(core):
        return jnp.where(core == 0, x, z)

    def halo_peer(k, sign):
        return ((fx + sign * (k // 4) + 8) % 8, (fy + sign * (k % 4) + 16) % 16)

    def plane_peer(k, sign):
        far = (jnp.where(first, z, x) + sign * (k // 4) + 4) % 4
        yy = (y + sign * (k % 4) + 4) % 4
        return device(jnp.where(first, x, far), yy, jnp.where(first, far, z), core), far * 4 + yy

    def last_peer(k, sign):
        other = (core + k % 2) % 2
        mover = core if sign == 1 else other
        place = (axis_of(mover) + sign * (k // 2) + 4) % 4
        xx, zz = jnp.where(mover == 0, place, x), jnp.where(mover == 0, z, place)
        slot = mover * 4 + (axis_of(mover) if sign == 1 else place)
        return device(xx, y, zz, other), slot

    barrier = pltpu.get_barrier_semaphore()
    for k in range(1, 12):
        pl.semaphore_signal(barrier, inc=1, device_id=halo_peer(k, -1), device_id_type=MESH)
    for k in range(1, 16):
        pl.semaphore_signal(barrier, inc=1, device_id=plane_peer(k, -1)[0], device_id_type=MESH)
    for k in range(1, 8):
        pl.semaphore_signal(barrier, inc=1, device_id=last_peer(k, -1)[0], device_id_type=MESH)
    pl.semaphore_wait(barrier, 33)

    def halo_copy(k):
        return pltpu.make_async_remote_copy(
            src_ref=pieces_ref.at[k], dst_ref=halo.at[k],
            send_sem=halo_sems.at[0, k], recv_sem=halo_sems.at[1, k],
            device_id=halo_peer(k, 1), device_id_type=MESH,
        )

    own = jnp.where(first, z, x) * 4 + y

    def plane_copy(k, slot):
        return pltpu.make_async_remote_copy(
            src_ref=plane.at[own], dst_ref=plane.at[slot],
            send_sem=plane_sems.at[0, k], recv_sem=plane_sems.at[1, k],
            device_id=plane_peer(k, 1)[0], device_id_type=MESH,
        )

    def last_copy(k, slot):
        return pltpu.make_async_remote_copy(
            src_ref=outbox.at[k], dst_ref=fin.at[slot],
            send_sem=last_sems.at[0, k], recv_sem=last_sems.at[1, k],
            device_id=last_peer(k, 1)[0], device_id_type=MESH,
        )

    for k in range(1, 12):
        halo_copy(k).start()
    total = pieces_ref[0].astype(F32)
    for k in range(1, 12):
        halo_copy(k).wait_recv()
        total = total + halo[k].astype(F32)
    plane[own] = total.astype(BF)
    for k in range(1, 16):
        plane_copy(k, own).start()
    for k in range(1, 16):
        plane_copy(k, plane_peer(k, -1)[1]).wait_recv()
    mine = core * 4 + axis_of(core)
    for k in range(1, 8):
        peer = last_peer(k, 1)[0]
        outbox[k] = plane[:, readers_ref[peer[0] * 16 + peer[1]]]
        last_copy(k, mine).start()
    fin[mine] = plane[:, readers_ref[fx * 16 + fy]]
    for k in range(1, 8):
        last_copy(k, last_peer(k, -1)[1]).wait_recv()
    for k in range(1, 12):
        halo_copy(k).wait_send()
    for k in range(1, 16):
        plane_copy(k, own).wait_send()
    for k in range(1, 8):
        last_copy(k, mine).wait_send()
    out_ref[...] = fin[...]


def exchange(pieces, readers):
    vmem = pl.BlockSpec(memory_space=pltpu.VMEM)
    return pl.pallas_call(
        exchange_kernel,
        out_shape=jax.ShapeDtypeStruct((8, 16, 32, 128), BF),
        in_specs=[vmem, pl.BlockSpec(memory_space=pltpu.SMEM)],
        out_specs=vmem,
        scratch_shapes=[
            pltpu.VMEM((12, NSUB, 32, 128), BF),
            pltpu.VMEM((16, NSUB, 32, 128), BF),
            pltpu.VMEM((8, 16, 32, 128), BF),
            pltpu.VMEM((8, 16, 32, 128), BF),
            pltpu.SemaphoreType.DMA((2, 12)),
            pltpu.SemaphoreType.DMA((2, 16)),
            pltpu.SemaphoreType.DMA((2, 8)),
        ],
        compiler_params=pltpu.CompilerParams(
            collective_id=0, has_side_effects=True, vmem_limit_bytes=32 * 2**20
        ),
    )(pieces, readers)


def place_of(i, j):
    x, y, z, core = 2 * (j // 8) + i % 2, i // 2, (j // 2) % 4, j % 2
    return (4 + z, x * 4 + y) if core else (x, z * 4 + y)


def turned(kernel, start):
    first = start & 7
    row = iota(kernel.shape, 0)
    laid = kernel
    for r in range(1, 8):
        laid = jnp.where(first == r, jnp.roll(kernel, r, 0), laid)
    return laid, (start >> 3) + jnp.where(row < first, 1, 0)


def degrid_kernel(fin_ref, cells_ref, rows_ref, cols_ref, et_ref, en_ref, out_ref, yy, grid_t):
    for j in range(0, 16, 2):
        lhs = []
        for i in range(8):
            at = [place_of(i, j + d) for d in range(2)]
            lhs.append(jnp.concatenate([fin_ref[a, b] for a, b in at], 0))
        done = jnp.dot(jnp.concatenate(lhs, 1), et_ref[...], preferred_element_type=F32).astype(BF)
        yy[32 * j : 32 * j + 64] = done[:, :SUB]
        yy[SUB + 32 * j : SUB + 32 * j + 64] = done[:, SUB:]

    @pl.loop(0, 8)
    def _(h):
        part = pl.ds(pl.multiple_of(h * 128, 128), 128)
        grid_t[part] = jnp.dot(en_ref[part], yy[...], preferred_element_type=F32).astype(BF)

    @pl.loop(0, cells_ref.shape[1] // VTILE)
    def _(t):
        at = pl.ds(pl.multiple_of(t * VTILE, VTILE), VTILE)
        taps, block = turned(rows_ref[:, at].astype(F32), cells_ref[0:1, at])
        across = iota((SUB // 8, 8, VTILE), 0)
        spread = jnp.where(across == block[None], taps[None], 0.0).reshape(SUB, VTILE).astype(BF)
        taps, block = turned(cols_ref[:, at], cells_ref[1:2, at])
        sums = [jnp.zeros((8, VTILE), F32), jnp.zeros((8, VTILE), F32)]
        for c in range(4):
            here = (iota((16, 8, VTILE), 0) + 16 * c) == block[None]
            for p in range(2):
                part = grid_t[SUB * p + 128 * c : SUB * p + 128 * c + 128]
                values = jnp.dot(part, spread, preferred_element_type=F32)
                values = values.reshape(16, 8, VTILE)
                sums[p] = sums[p] + jnp.sum(jnp.where(here, values, 0.0), axis=0)
        for p in range(2):
            out_ref[p : p + 1, at] = jnp.sum(sums[p] * taps, axis=0, keepdims=True)


def degrid(fin, vis_cells, row_kernel, col_kernel):
    vmem = pl.BlockSpec(memory_space=pltpu.VMEM)
    return pl.pallas_call(
        degrid_kernel,
        out_shape=jax.ShapeDtypeStruct((2, vis_cells.shape[1]), F32),
        in_specs=[vmem] * 6,
        out_specs=vmem,
        scratch_shapes=[
            pltpu.VMEM((2 * SUB, SUB), BF),
            pltpu.VMEM((2 * SUB, SUB), BF),
        ],
        compiler_params=pltpu.CompilerParams(vmem_limit_bytes=32 * 2**20),
    )(fin, vis_cells, row_kernel, col_kernel, *grid_tables())


def local(sky, sub_off, readers, vis_cells, row_kernel, col_kernel):
    pieces = facets(sky, sub_off)
    fin = exchange(pieces, readers)
    return degrid(fin, vis_cells, row_kernel, col_kernel)


def solution(mesh):
    return jax.shard_map(
        local,
        mesh=mesh,
        in_specs=(
            P("fx", "fy"),
            P(),
            P(),
            P(None, ("fx", "fy")),
            P(None, ("fx", "fy")),
            P(None, ("fx", "fy")),
        ),
        out_specs=P(None, ("fx", "fy")),
        check_vma=False,
    )
```

time: 468 us -> 73.6 us (0.16); the launches traced: 460 us -> 73.3 us
  waiting for transfers between devices: 182 us -> 0 us
  blocking collectives: 114 us -> 0 us
  other arithmetic: 66.8 us -> 0 us
  Pallas kernels: 0 us -> 65.3 us
  matrix products: 51.9 us -> 0 us
  local copies, waits for them, and re-layouts: 28.9 us -> 7.88 us
  between operations: 16.1 us -> 0.09 us
    all_gather x1 -> x0, waiting for transfers between devices: 182 us -> none  [local(): whole = lax.all_gather(piece, ('fx', 'fy'), axis=0, tiled=True)]
    unnamed x1 -> x0, blocking collectives: 114 us -> none
    pallas_call x0 -> x3, Pallas kernels: none -> 65.3 us  [the longest x1 35.4 us: exchange(): pl.pallas_call(exchange_kernel, out_shape=jax.ShapeDtypeStruct((8, 16, 32...]
    dot_general x13 -> x0, matrix products: 51.9 us -> none  [the longest x1 10.1 us: local(): jnp.dot(sky, strip_table(sub_off[1], col_start, sky_cells), preferred_ele...]
    cos x1 -> x0, other arithmetic: 48.4 us -> none  [strip_table(): jnp.cos(angles)]
    another operation x5 -> x0, other arithmetic: 11 us -> none
    transpose x1 -> x0, local copies, waits for them, and re-layouts: 10.3 us -> none  [local(): jnp.einsum('mcsl,cdnl->mdsn', partial_rows, col_table, precision=lax.Prec...]
    add x3 -> x0, other arithmetic: 5.82 us -> none  [the longest x1 5.75 us: degridding(): col_weights + jnp.where(col_gap == tap_index, col_kernel[tap_index][:, No...]
  transfers between devices with their start and end apart: 1 -> 0, of which waited for: 1 -> 0; matrix products, arithmetic and copies ran while one was open for 3% -> 0% of each run, Pallas kernels for 0% -> 0%
where the time goes in v1:
time: 73.6 us; the launch traced here: 73.3 us
  Pallas kernels  65.3 us (89%)
  local copies, waits for them, and re-layouts  7.88 us (11%)
    pallas_call x1, Pallas kernels, exchange(): pl.pallas_call(exchange_kernel, out_shape=jax.ShapeDtypeStruct((8, 16, 32...  35.4 us
    pallas_call x1, Pallas kernels, facets(): pl.pallas_call(facet_kernel, out_shape=jax.ShapeDtypeStruct((12, NSUB, 32...  20 us
    pallas_call x1, Pallas kernels, degrid(): pl.pallas_call(degrid_kernel, out_shape=jax.ShapeDtypeStruct((2, vis_cell...  9.97 us
    unnamed x24, local copies, waits for them, and re-layouts  7.88 us

profile of v1, /device:TPU:1, one launch (start us, length us, event | category | flops | bytes accessed | tf_op | source)
XLA Modules:
  0.0 73.3 jit_solution(588385792719969702)
XLA Ops:
  0.0 0.0 copy-start
  0.0 3.4 %copy-done = bf16[1024,4096]{1,0:T(8,128)(2,1)S(1)} copy-done((bf16[1024,4096]{1,0:T(8,128)(2,1)S(1)}, bf16[1024,4096]{1,0:T(8,128)(2,1)}, u32[]{:S(2)}) %copy-start) | copy-done | bytes 8388632
  3.4 0.0 copy-start.3
  3.4 1.0 %copy-done.3 = bf16[512,384]{1,0:T(8,128)(2,1)S(1)} copy-done((bf16[512,384]{1,0:T(8,128)(2,1)S(1)}, bf16[512,384]{1,0:T(8,128)(2,1)}, u32[]{:S(2)}) %copy-start.3) | copy-done | bytes 393240
  4.4 0.0 copy-start.4
  4.4 0.9 %copy-done.4 = f32[128,512]{1,0:T(8,128)S(1)} copy-done((f32[128,512]{1,0:T(8,128)S(1)}, f32[128,512]{1,0:T(8,128)}, u32[]{:S(2)}) %copy-start.4) | copy-done | bytes 262168
  5.3 0.0 copy-start.5
  5.3 0.9 %copy-done.5 = f32[128,512]{1,0:T(8,128)S(1)} copy-done((f32[128,512]{1,0:T(8,128)S(1)}, f32[128,512]{1,0:T(8,128)}, u32[]{:S(2)}) %copy-start.5) | copy-done | bytes 262168
  6.3 0.0 copy-start.6
  6.3 0.9 %copy-done.6 = bf16[256,256]{1,0:T(8,128)(2,1)S(1)} copy-done((bf16[256,256]{1,0:T(8,128)(2,1)S(1)}, bf16[256,256]{1,0:T(8,128)(2,1)}, u32[]{:S(2)}) %copy-start.6) | copy-done | bytes 131096
  7.2 0.7 copy-done.10
  7.9 0.0 copy-start.11
  7.9 0.0 copy-start.1
  7.9 0.0 copy-start.8
  7.9 0.0 copy-start.9
  7.9 20.0 %shard_map.118.pieces_ref = bf16[12,4,32,128]{3,2,1,0:T(8,128)(2,1)S(1)} custom-call(bf16[1024,4096]{1,0:T(8,128)(2,1)S(1)} %copy-done, s32[2,4]{1,0:T(2,128)S(1)} %copy-done.10, bf16[256,256]{1,0:T(8,128)(2,1)S(1)} %copy-done.6, bf16[512,384]{1,0:T(8,128)(2,1)S(1)} %copy-done.3, f32[128,512]{1,0:T(8,128)S(1)} %copy-done.5, f32[128,512]{1,0:T(8,128)S(1)} %copy-done.4), custom_call_target="tpu_custom_call" | custom-call | tf_op jit(solution)/shard_map/pallas_call | solution.py:162
  27.9 0.0 copy-done.11
  27.9 35.4 %shard_map.119.fin_ref = bf16[8,16,32,128]{3,2,1,0:T(8,128)(2,1)S(1)} custom-call(bf16[12,4,32,128]{3,2,1,0:T(8,128)(2,1)S(1)} %shard_map.118.pieces_ref, s32[128]{0:T(128)S(1)} %copy-done.11), custom_call_target="tpu_custom_call" | custom-call | tf_op jit(solution)/shard_map/pallas_call | solution.py:274
  63.3 0.0 copy-done.1
  63.3 0.0 copy-done.2
  63.3 0.0 copy-done.7
  63.3 0.0 copy-done.8
  63.3 0.0 copy-done.9
  63.3 10.0 %shard_map.120 = f32[2,2048]{1,0:T(2,128)} custom-call(bf16[8,16,32,128]{3,2,1,0:T(8,128)(2,1)S(1)} %shard_map.119.fin_ref, s32[2,2048]{1,0:T(2,128)S(1)} %copy-done.9, bf16[8,2048]{1,0:T(8,128)(2,1)S(1)} %copy-done.8, f32[8,2048]{1,0:T(8,128)S(1)} %copy-done.7, bf16[1024,1024]{1,0:T(8,128)(2,1)S(1)} %copy-done.2, bf16[1024,1024]{1,0:T(8,128)(2,1)S(1)} %copy-done.1), custom_call_target="tpu_custom_call" | custom-call | tf_op jit(solution)/shard_map/pallas_call | solution.py:344
  (3 shorter events, 0.0 us)
Async XLA Ops:
  0.0 3.4 %copy-start = (bf16[1024,4096]{1,0:T(8,128)(2,1)S(1)}, bf16[1024,4096]{1,0:T(8,128)(2,1)}, u32[]{:S(2)}) copy-start(bf16[1024,4096]{1,0:T(8,128)(2,1)} %sky_ref.1) | copy-start | bytes 25165828
  3.4 1.0 %copy-start.3 = (bf16[512,384]{1,0:T(8,128)(2,1)S(1)}, bf16[512,384]{1,0:T(8,128)(2,1)}, u32[]{:S(2)}) copy-start(bf16[512,384]{1,0:T(8,128)(2,1)} %constant.13.clone.dr_ref) | copy-start | bytes 1179652
  4.4 0.9 %copy-start.4 = (f32[128,512]{1,0:T(8,128)S(1)}, f32[128,512]{1,0:T(8,128)}, u32[]{:S(2)}) copy-start(f32[128,512]{1,0:T(8,128)} %constant.15.clone.qim_ref) | copy-start | bytes 786436
  5.3 0.9 %copy-start.5 = (f32[128,512]{1,0:T(8,128)S(1)}, f32[128,512]{1,0:T(8,128)}, u32[]{:S(2)}) copy-start(f32[128,512]{1,0:T(8,128)} %constant.14.clone.qre_ref) | copy-start | bytes 786436
  6.3 0.9 %copy-start.6 = (bf16[256,256]{1,0:T(8,128)(2,1)S(1)}, bf16[256,256]{1,0:T(8,128)(2,1)}, u32[]{:S(2)}) copy-start(bf16[256,256]{1,0:T(8,128)(2,1)} %constant.12.clone.dc_ref) | copy-start | bytes 393220
  7.2 0.7 copy-start.10
  7.9 20.0 %copy-start.11 = (s32[128]{0:T(128)S(1)}, s32[128]{0:T(128)}, u32[]{:S(2)}) copy-start(s32[128]{0:T(128)} %readers_ref.1) | copy-start | bytes 1540
  7.9 55.4 %copy-start.1 = (bf16[1024,1024]{1,0:T(8,128)(2,1)S(1)}, bf16[1024,1024]{1,0:T(8,128)(2,1)}, u32[]{:S(2)}) copy-start(bf16[1024,1024]{1,0:T(8,128)(2,1)} %constant.17.clone.en_ref) | copy-start | bytes 6291460
  7.9 55.4 %copy-start.2 = (bf16[1024,1024]{1,0:T(8,128)(2,1)S(1)}, bf16[1024,1024]{1,0:T(8,128)(2,1)}, u32[]{:S(2)}) copy-start(bf16[1024,1024]{1,0:T(8,128)(2,1)} %constant.16.clone.et_ref) | copy-start | bytes 6291460
  7.9 55.4 %copy-start.7 = (f32[8,2048]{1,0:T(8,128)S(1)}, f32[8,2048]{1,0:T(8,128)}, u32[]{:S(2)}) copy-start(f32[8,2048]{1,0:T(8,128)} %cols_ref.1) | copy-start | bytes 196612
  7.9 55.5 %copy-start.8 = (bf16[8,2048]{1,0:T(8,128)(2,1)S(1)}, bf16[8,2048]{1,0:T(8,128)(2,1)}, u32[]{:S(2)}) copy-start(bf16[8,2048]{1,0:T(8,128)(2,1)} %rows_ref.1) | copy-start | bytes 98308
  7.9 55.5 %copy-start.9 = (s32[2,2048]{1,0:T(2,128)S(1)}, s32[2,2048]{1,0:T(2,128)}, u32[]{:S(2)}) copy-start(s32[2,2048]{1,0:T(2,128)} %cells_ref.1) | copy-start | bytes 49156

commit v2 on v1

v2 whole, which is shorter than its diff:
```python
import math

import jax
import jax.numpy as jnp
import numpy as np
from jax import lax
from jax.experimental import pallas as pl
from jax.experimental.pallas import tpu as pltpu
from jax.sharding import PartitionSpec as P

FACET = 4096
SUB = 512
K = 128
W = 8
FR = 512
NSUB = 4
SKY = 65536
CHUNK = 512
CHUNKS = FACET // CHUNK
VTILE = 256
BF = jnp.bfloat16
F32 = jnp.float32
MESH = pl.DeviceIdType.MESH


def wave(rows, cols, period):
    turn = (np.arange(rows)[:, None] * np.arange(cols)[None, :]) % period
    angle = turn * (2.0 * math.pi / period)
    return np.cos(angle), np.sin(angle)


def small_tables():
    re, im = wave(K, K, K)
    re, im = re / K, -im / K
    cols = np.block([[re.T, im.T], [-im.T, re.T]])
    rows = np.zeros((2, 2, K, 3, 2, 64))
    for f in range(2):
        for t in range(K):
            at, cell = divmod(32 * f + t, 64)
            rows[f, 0, :, at, 0, cell] = re[t]
            rows[f, 1, :, at, 0, cell] = -im[t]
            rows[f, 0, :, at, 1, cell] = im[t]
            rows[f, 1, :, at, 1, cell] = re[t]
    qre, qim = wave(K, FR, SKY // 4)
    scale = 1.0 / math.sqrt(FR)
    return (
        jnp.asarray(cols, BF),
        jnp.asarray(rows.reshape(4 * K, 384), BF),
        jnp.asarray(qre * scale, F32),
        jnp.asarray(-qim * scale, F32),
    )


def grid_tables():
    re, im = wave(SUB, SUB, SUB)
    et = np.stack([np.concatenate([re, im], 1), np.concatenate([-im, re], 1)])
    et = et.reshape(2, 8, 64, 2 * SUB).transpose(1, 0, 2, 3).reshape(2 * SUB, 2 * SUB)
    en = np.block([[re, -im], [im, re]]) / 16.0
    return jnp.asarray(et, BF), jnp.asarray(en, BF)


def cis(phase):
    turn = phase & 0xFFFF
    quarter = (turn + 8192) >> 14
    x = (turn - (quarter << 14)).astype(F32) * (2.0 * math.pi / SKY)
    x2 = x * x
    c = 1.0 + x2 * (-0.5 + x2 * (1.0 / 24 + x2 * (-1.0 / 720 + x2 * (1.0 / 40320))))
    s = x * (1.0 + x2 * (-1.0 / 6 + x2 * (1.0 / 120 + x2 * (-1.0 / 5040 + x2 * (1.0 / 362880)))))
    odd = (quarter & 1) == 1
    cos = jnp.where(odd, s, c)
    sin = jnp.where(odd, c, s)
    cos = jnp.where(((quarter + 1) & 2) != 0, -cos, cos)
    sin = jnp.where((quarter & 2) != 0, -sin, sin)
    return cos, sin


def iota(shape, dim):
    return lax.broadcasted_iota(jnp.int32, shape, dim)


def turned(kernel, start):
    first = start & 7
    row = iota(kernel.shape, 0)
    laid = kernel
    for r in range(1, 8):
        laid = jnp.where(first == r, jnp.roll(kernel, r, 0), laid)
    return laid, (start >> 3) + jnp.where(row < first, 1, 0)


def place_of(i, j):
    j = (j + 15) % 16
    x, y, z, core = 2 * (j // 8) + i % 2, i // 2, (j // 2) % 4, j % 2
    return (4 + z, x * 4 + y) if core else (x, z * 4 + y)


def kernel(
    sky_ref, off_ref, readers_ref, cells_ref, rows_ref, cols_ref,
    dc_ref, dr_ref, qre_ref, qim_ref, et_ref, en_ref, out_ref,
    sky_v, va, vb, acc, coarse, fine, uu, pieces, halo, plane, outbox, fin,
    lhs, yy, grid_t, spread, taps, blocks, et, en, dc, dr, qre_v, qim_v, cells, rows, cols,
    sky_sems, load_sems, halo_sems, plane_sems, last_sems,
):
    fx, fy = lax.axis_index("fx"), lax.axis_index("fy")
    y, core, z = fx // 2, fy % 2, (fy // 2) % 4
    x = 2 * (fy // 8) + fx % 2
    first = core == 0

    def sky_copy(c):
        part = pl.ds(c * CHUNK, CHUNK)
        return pltpu.make_async_copy(sky_ref.at[:, part], sky_v.at[:, part], sky_sems.at[c])

    moves = [
        (dc_ref, dc), (dr_ref, dr), (qre_ref, qre_v), (qim_ref, qim_v),
        (cells_ref, cells), (rows_ref, rows), (cols_ref, cols), (et_ref, et), (en_ref, en),
    ]
    loads = [
        pltpu.make_async_copy(src, dst, load_sems.at[n]) for n, (src, dst) in enumerate(moves)
    ]
    for c in range(CHUNKS):
        sky_copy(c).start()
    for load in loads:
        load.start()

    def device(x, y, z, core):
        return (2 * y + x % 2, (x // 2) * 8 + 2 * z + core)

    def axis_of(core):
        return jnp.where(core == 0, x, z)

    def halo_peer(k, sign):
        return ((fx + sign * (k // 4) + 8) % 8, (fy + sign * (k % 4 - 1) + 16) % 16)

    def plane_peer(k, sign):
        far = (jnp.where(first, z, x) + sign * (k // 4) + 4) % 4
        yy = (y + sign * (k % 4) + 4) % 4
        return device(jnp.where(first, x, far), yy, jnp.where(first, far, z), core), far * 4 + yy

    def last_peer(k, sign):
        other = (core + k % 2) % 2
        mover = core if sign == 1 else other
        place = (axis_of(mover) + sign * (k // 2) + 4) % 4
        xx, zz = jnp.where(mover == 0, place, x), jnp.where(mover == 0, z, place)
        slot = mover * 4 + (axis_of(mover) if sign == 1 else place)
        return device(xx, y, zz, other), slot

    halo_ks = [k for k in range(12) if k != 1]
    barrier = pltpu.get_barrier_semaphore()
    for k in halo_ks:
        pl.semaphore_signal(barrier, inc=1, device_id=halo_peer(k, -1), device_id_type=MESH)
    for k in range(1, 16):
        pl.semaphore_signal(barrier, inc=1, device_id=plane_peer(k, -1)[0], device_id_type=MESH)
    for k in range(1, 8):
        pl.semaphore_signal(barrier, inc=1, device_id=last_peer(k, -1)[0], device_id_type=MESH)

    own = jnp.where(first, z, x) * 4 + y
    mine = core * 4 + axis_of(core)

    def halo_copy(s, k):
        return pltpu.make_async_remote_copy(
            src_ref=pieces.at[s, k], dst_ref=halo.at[s, k],
            send_sem=halo_sems.at[0, s, k], recv_sem=halo_sems.at[1, s, k],
            device_id=halo_peer(k, 1), device_id_type=MESH,
        )

    def plane_copy(s, k, slot):
        return pltpu.make_async_remote_copy(
            src_ref=plane.at[s, own], dst_ref=plane.at[s, slot],
            send_sem=plane_sems.at[0, s, k], recv_sem=plane_sems.at[1, s, k],
            device_id=plane_peer(k, 1)[0], device_id_type=MESH,
        )

    def last_copy(k, slot):
        return pltpu.make_async_remote_copy(
            src_ref=outbox.at[k], dst_ref=fin.at[slot],
            send_sem=last_sems.at[0, k], recv_sem=last_sems.at[1, k],
            device_id=last_peer(k, 1)[0], device_id_type=MESH,
        )

    step, lane = iota((64, K), 0), iota((64, K), 1)
    for s in range(NSUB):
        freq = off_ref[1, s] + 4 * lane
        cos, sin = cis(freq * (64 * step + FACET * fy) + SKY // 4 * lane * fy)
        coarse[s, 0] = cos
        coarse[s, 1] = -sin
        cos, sin = cis(freq * step)
        fine[s, 0] = cos * (1.0 / 64)
        fine[s, 1] = -sin * (1.0 / 64)

    def fill(s, h, ref):
        bre, bim = fine[s, 0], fine[s, 1]
        are, aim = coarse[s, 0, pl.ds(h, 1), :], coarse[s, 1, pl.ds(h, 1), :]
        at = pl.ds(pl.multiple_of(h * 64, 64), 64)
        ref[at, 0:K] = (are * bre - aim * bim).astype(BF)
        ref[at, K : 2 * K] = (are * bim + aim * bre).astype(BF)

    def strips_of(s, table, after):
        if s == 0:
            for c in range(0, CHUNKS, 2):
                sky_copy(c).wait()
                sky_copy(c + 1).wait()
                part = slice(c * CHUNK, (c + 2) * CHUNK)
                added = jnp.dot(sky_v[:, part], table[part], preferred_element_type=F32)
                acc[...] = added if c == 0 else acc[...] + added
                for h in range(8 * c, 8 * c + 16):
                    fill(s + 1, h, after)
        else:

            @pl.loop(0, 2)
            def _(t):
                part = pl.ds(pl.multiple_of(t * FR, FR), FR)
                acc[part] = jnp.dot(sky_v[part, :], table[...], preferred_element_type=F32)
                if s + 1 < NSUB:
                    for h in range(32):
                        fill(s + 1, 32 * t + h, after)

    def window_of(s):
        places = iota((1, FR), 1)
        parts = []
        for f in range(2):
            cos, sin = cis(off_ref[0, s] * (FACET * (2 * fx + f) + places))
            qre, qim = qre_v[...], qim_v[...]
            ure, uim = qre * cos + qim * sin, qim * cos - qre * sin
            if f == 1:
                sign = jnp.where((iota((K, 1), 0) & 1) == 1, -1.0, 1.0)
                ure, uim = ure * sign, uim * sign
            uu[0:K] = ure.astype(BF)
            uu[K : 2 * K] = uim.astype(BF)
            strips = acc[FR * f : FR * (f + 1)].astype(BF)
            mixed = jnp.dot(uu[...], strips, preferred_element_type=F32)
            bre = mixed[:K, :K] - mixed[K:, K:]
            bim = mixed[:K, K:] + mixed[K:, :K]
            block = jnp.concatenate([bre, bim], 1).astype(BF)
            image = jnp.dot(block, dc[...], preferred_element_type=F32)
            parts += [image[:, :K].T.astype(BF), image[:, K:].T.astype(BF)]
        window = jnp.dot(jnp.concatenate(parts, 1), dr[...], preferred_element_type=F32)
        window = window.astype(BF)
        for di in range(3):
            for dj in range(4):
                pieces[s, di * 4 + dj] = window[32 * dj : 32 * dj + 32, 128 * di : 128 * di + 128]

    def sum_halo(s):
        total = pieces[s, 1].astype(F32)
        for k in halo_ks:
            halo_copy(s, k).wait_recv()
            total = total + halo[s, k].astype(F32)
        plane[s, own] = total.astype(BF)
        for k in range(1, 16):
            plane_copy(s, k, own).start()

    @pl.loop(0, 64)
    def _(h):
        fill(0, h, va)

    for s in range(NSUB):
        table, after = (va, vb) if s % 2 == 0 else (vb, va)
        strips_of(s, table, after)
        if s == 0:
            for load in loads[:4]:
                load.wait()
        window_of(s)
        if s == 0:
            pl.semaphore_wait(barrier, 33)
        for k in halo_ks:
            halo_copy(s, k).start()
        if s >= 2:
            sum_halo(s - 2)

    for load in loads[4:]:
        load.wait()
    tiles = cells.shape[1] // VTILE

    @pl.loop(0, tiles)
    def _(t):
        at = pl.ds(pl.multiple_of(t * VTILE, VTILE), VTILE)
        laid, block = turned(rows[:, at].astype(F32), cells[0:1, at])
        across = iota((SUB // 8, 8, VTILE), 0)
        weights = jnp.where(across == block[None], laid[None], 0.0)
        spread[:, at] = weights.reshape(SUB, VTILE).astype(BF)
        laid, block = turned(cols[:, at], cells[1:2, at])
        taps[:, at] = laid
        blocks[:, at] = block

    sum_halo(2)
    sum_halo(3)
    for s in range(NSUB):
        for k in range(1, 16):
            plane_copy(s, k, plane_peer(k, -1)[1]).wait_recv()
    for k in range(1, 8):
        peer = last_peer(k, 1)[0]
        outbox[k] = plane[readers_ref[peer[0] * 16 + peer[1]]]
        last_copy(k, mine).start()
    fin[mine] = plane[readers_ref[fx * 16 + fy]]
    for k in range(1, 8):
        last_copy(k, last_peer(k, -1)[1]).wait_recv()

    for i in range(8):
        for j in range(16):
            a, b = place_of(i, j)
            lhs[32 * j : 32 * j + 32, 128 * i : 128 * i + 128] = fin[a, b]
    for h in range(2):
        at = slice(SUB * h, SUB * h + SUB)
        yy[at] = jnp.dot(lhs[...], et[:, at], preferred_element_type=F32).astype(BF)
    for h in range(2):
        at = slice(SUB * h, SUB * h + SUB)
        grid_t[at] = jnp.dot(en[at], yy[...], preferred_element_type=F32).astype(BF)

    @pl.loop(0, tiles)
    def _(t):
        at = pl.ds(pl.multiple_of(t * VTILE, VTILE), VTILE)
        block = blocks[:, at]
        sums = [jnp.zeros((8, VTILE), F32), jnp.zeros((8, VTILE), F32)]
        for c in range(4):
            here = (iota((16, 8, VTILE), 0) + 16 * c) == block[None]
            for p in range(2):
                part = grid_t[SUB * p + 128 * c : SUB * p + 128 * c + 128]
                values = jnp.dot(part, spread[:, at], preferred_element_type=F32)
                values = values.reshape(16, 8, VTILE)
                sums[p] = sums[p] + jnp.sum(jnp.where(here, values, 0.0), axis=0)
        for p in range(2):
            out_ref[p : p + 1, at] = jnp.sum(sums[p] * taps[:, at], axis=0, keepdims=True)

    for s in range(NSUB):
        for k in halo_ks:
            halo_copy(s, k).wait_send()
        for k in range(1, 16):
            plane_copy(s, k, own).wait_send()
    for k in range(1, 8):
        last_copy(k, mine).wait_send()


def local(sky, sub_off, readers, vis_cells, row_kernel, col_kernel):
    hbm = pl.BlockSpec(memory_space=pltpu.HBM)
    smem = pl.BlockSpec(memory_space=pltpu.SMEM)
    count = vis_cells.shape[1]
    return pl.pallas_call(
        kernel,
        out_shape=jax.ShapeDtypeStruct((2, count), F32),
        in_specs=[hbm, smem, smem] + [hbm] * 9,
        out_specs=pl.BlockSpec(memory_space=pltpu.VMEM),
        scratch_shapes=[
            pltpu.VMEM((2 * FR, FACET), BF),
            pltpu.VMEM((FACET, 2 * K), BF),
            pltpu.VMEM((FACET, 2 * K), BF),
            pltpu.VMEM((2 * FR, 2 * K), F32),
            pltpu.VMEM((NSUB, 2, 64, K), F32),
            pltpu.VMEM((NSUB, 2, 64, K), F32),
            pltpu.VMEM((2 * K, FR), BF),
            pltpu.VMEM((NSUB, 12, 32, 128), BF),
            pltpu.VMEM((NSUB, 12, 32, 128), BF),
            pltpu.VMEM((NSUB, 16, 32, 128), BF),
            pltpu.VMEM((8, 16, 32, 128), BF),
            pltpu.VMEM((8, 16, 32, 128), BF),
            pltpu.VMEM((SUB, 2 * SUB), BF),
            pltpu.VMEM((2 * SUB, SUB), BF),
            pltpu.VMEM((2 * SUB, SUB), BF),
            pltpu.VMEM((SUB, count), BF),
            pltpu.VMEM((8, count), F32),
            pltpu.VMEM((8, count), jnp.int32),
            pltpu.VMEM((2 * SUB, 2 * SUB), BF),
            pltpu.VMEM((2 * SUB, 2 * SUB), BF),
            pltpu.VMEM((2 * K, 2 * K), BF),
            pltpu.VMEM((4 * K, 384), BF),
            pltpu.VMEM((K, FR), F32),
            pltpu.VMEM((K, FR), F32),
            pltpu.VMEM((2, count), jnp.int32),
            pltpu.VMEM((8, count), BF),
            pltpu.VMEM((8, count), F32),
            pltpu.SemaphoreType.DMA((CHUNKS,)),
            pltpu.SemaphoreType.DMA((9,)),
            pltpu.SemaphoreType.DMA((2, NSUB, 12)),
            pltpu.SemaphoreType.DMA((2, NSUB, 16)),
            pltpu.SemaphoreType.DMA((2, 8)),
        ],
        compiler_params=pltpu.CompilerParams(
            collective_id=0, has_side_effects=True, vmem_limit_bytes=56 * 2**20
        ),
    )(sky, sub_off, readers, vis_cells, row_kernel, col_kernel, *small_tables(), *grid_tables())


def solution(mesh):
    return jax.shard_map(
        local,
        mesh=mesh,
        in_specs=(
            P("fx", "fy"),
            P(),
            P(),
            P(None, ("fx", "fy")),
            P(None, ("fx", "fy")),
            P(None, ("fx", "fy")),
        ),
        out_specs=P(None, ("fx", "fy")),
        check_vma=False,
    )
```

time: 73.6 us -> 54.5 us (0.74)
  Pallas kernels: 65.3 us -> 53 us
  local copies, waits for them, and re-layouts: 7.88 us -> 1.32 us
    pallas_call x3 -> x1, Pallas kernels: 65.3 us -> 53 us  [local(): pl.pallas_call(kernel, out_shape=jax.ShapeDtypeStruct((2, count), F32), i...]
    unnamed x24 -> x1, local copies, waits for them, and re-layouts: 7.88 us -> 1.32 us
where the time goes in v2:
time: 54.5 us; the launch traced here: 54.3 us
  Pallas kernels  53 us (97%)
  local copies, waits for them, and re-layouts  1.32 us (2%)
    pallas_call x1, Pallas kernels, local(): pl.pallas_call(kernel, out_shape=jax.ShapeDtypeStruct((2, count), F32), i...  53 us
    unnamed x1, local copies, waits for them, and re-layouts  1.32 us

profile of v2, /device:TPU:1, one launch (start us, length us, event | category | flops | bytes accessed | tf_op | source)
XLA Modules:
  0.0 54.3 jit_solution(17704805384397360653)
XLA Ops:
  0.0 53.0 %shard_map.118 = f32[2,2048]{1,0:T(2,128)} custom-call(bf16[1024,4096]{1,0:T(8,128)(2,1)} %sky_ref.1, s32[2,4]{1,0:T(2,128)} %off_ref.1, s32[128]{0:T(128)} %readers_ref.1, s32[2,2048]{1,0:T(2,128)} %cells_ref.1, bf16[8,2048]{1,0:T(8,128)(2,1)} %rows_ref.1, f32[8,2048]{1,0:T(8,128)} %cols_ref.1, bf16[256,256]{1,0:T(8,128)(2,1)} %constant.12.clone.dc_ref, ...), custom_call_target="tpu_custom_call" | custom-call | tf_op jit(solution)/shard_map/pallas_call | solution.py:335
  53.0 1.3 %copy.14 = f32[2,2048]{1,0:T(2,128)} copy(f32[2,2048]{1,0:T(2,128)} %shard_map.118) | data formatting | bytes 32768

commit v3 on v2

--- a/solution.py
+++ b/solution.py
@@ -15,8 +15,8 @@
 FR = 512
 NSUB = 4
 SKY = 65536
-CHUNK = 512
-CHUNKS = FACET // CHUNK
+CHUNK = 256
+CHUNKS = 2 * FR // CHUNK
 VTILE = 256
 BF = jnp.bfloat16
 F32 = jnp.float32
@@ -96,9 +96,9 @@
 def kernel(
     sky_ref, off_ref, readers_ref, cells_ref, rows_ref, cols_ref,
     dc_ref, dr_ref, qre_ref, qim_ref, et_ref, en_ref, out_ref,
-    sky_v, va, vb, acc, coarse, fine, uu, pieces, halo, plane, outbox, fin,
+    sky_v, va, vb, acc, coarse, fine, images, pieces, halo, plane, outbox, fin,
     lhs, yy, grid_t, spread, taps, blocks, et, en, dc, dr, qre_v, qim_v, cells, rows, cols,
-    sky_sems, load_sems, halo_sems, plane_sems, last_sems,
+    sky_sems, load_sems, send_sems, halo_sems, plane_sems, last_sems,
 ):
     fx, fy = lax.axis_index("fx"), lax.axis_index("fy")
     y, core, z = fx // 2, fy % 2, (fy // 2) % 4
@@ -107,7 +107,7 @@
 
     def sky_copy(c):
         part = pl.ds(c * CHUNK, CHUNK)
-        return pltpu.make_async_copy(sky_ref.at[:, part], sky_v.at[:, part], sky_sems.at[c])
+        return pltpu.make_async_copy(sky_ref.at[part], sky_v.at[part], sky_sems.at[c])
 
     moves = [
         (dc_ref, dc), (dr_ref, dr), (qre_ref, qre_v), (qim_ref, qim_v),
@@ -144,6 +144,9 @@
         return device(xx, y, zz, other), slot
 
     halo_ks = [k for k in range(12) if k != 1]
+    halo_to = [halo_peer(k, 1) for k in halo_ks]
+    plane_to = [plane_peer(k, 1)[0] for k in range(1, 16)]
+    last_to = [last_peer(k, 1)[0] for k in range(1, 8)]
     barrier = pltpu.get_barrier_semaphore()
     for k in halo_ks:
         pl.semaphore_signal(barrier, inc=1, device_id=halo_peer(k, -1), device_id_type=MESH)
@@ -158,23 +161,26 @@
     def halo_copy(s, k):
         return pltpu.make_async_remote_copy(
             src_ref=pieces.at[s, k], dst_ref=halo.at[s, k],
-            send_sem=halo_sems.at[0, s, k], recv_sem=halo_sems.at[1, s, k],
-            device_id=halo_peer(k, 1), device_id_type=MESH,
+            send_sem=send_sems.at[0], recv_sem=halo_sems.at[s],
+            device_id=halo_to[k], device_id_type=MESH,
         )
 
-    def plane_copy(s, k, slot):
+    def plane_copy(s, k):
         return pltpu.make_async_remote_copy(
-            src_ref=plane.at[s, own], dst_ref=plane.at[s, slot],
-            send_sem=plane_sems.at[0, s, k], recv_sem=plane_sems.at[1, s, k],
-            device_id=plane_peer(k, 1)[0], device_id_type=MESH,
+            src_ref=plane.at[s, own], dst_ref=plane.at[s, own],
+            send_sem=send_sems.at[1], recv_sem=plane_sems.at[s],
+            device_id=plane_to[k], device_id_type=MESH,
         )
 
     def last_copy(k, slot):
         return pltpu.make_async_remote_copy(
             src_ref=outbox.at[k], dst_ref=fin.at[slot],
-            send_sem=last_sems.at[0, k], recv_sem=last_sems.at[1, k],
-            device_id=last_peer(k, 1)[0], device_id_type=MESH,
+            send_sem=send_sems.at[2], recv_sem=last_sems.at[k],
+            device_id=last_to[k], device_id_type=MESH,
         )
+
+    def wait_for(sem, ref):
+        pltpu.make_async_copy(ref, ref, sem).wait()
 
     step, lane = iota((64, K), 0), iota((64, K), 1)
     for s in range(NSUB):
@@ -193,77 +199,74 @@
         ref[at, 0:K] = (are * bre - aim * bim).astype(BF)
         ref[at, K : 2 * K] = (are * bim + aim * bre).astype(BF)
 
-    def strips_of(s, table, after):
-        if s == 0:
-            for c in range(0, CHUNKS, 2):
-                sky_copy(c).wait()
-                sky_copy(c + 1).wait()
-                part = slice(c * CHUNK, (c + 2) * CHUNK)
-                added = jnp.dot(sky_v[:, part], table[part], preferred_element_type=F32)
-                acc[...] = added if c == 0 else acc[...] + added
-                for h in range(8 * c, 8 * c + 16):
-                    fill(s + 1, h, after)
-        else:
-
-            @pl.loop(0, 2)
-            def _(t):
-                part = pl.ds(pl.multiple_of(t * FR, FR), FR)
-                acc[part] = jnp.dot(sky_v[part, :], table[...], preferred_element_type=F32)
-                if s + 1 < NSUB:
-                    for h in range(32):
-                        fill(s + 1, 32 * t + h, after)
+    def image_of(s, f):
+        cos, sin = cis(off_ref[0, s] * (FACET * (2 * fx + f) + iota((1, FR), 1)))
+        qre, qim = qre_v[...], qim_v[...]
+        ure, uim = qre * cos + qim * sin, qim * cos - qre * sin
+        if f == 1:
+            sign = jnp.where((iota((K, 1), 0) & 1) == 1, -1.0, 1.0)
+            ure, uim = ure * sign, uim * sign
+        table = jnp.concatenate([ure, uim], 0).astype(BF)
+        strips = acc[f].astype(BF)
+        mixed = jnp.dot(table, strips, preferred_element_type=F32)
+        bre = mixed[:K, :K] - mixed[K:, K:]
+        bim = mixed[:K, K:] + mixed[K:, :K]
+        block = jnp.concatenate([bre, bim], 1).astype(BF)
+        image = jnp.dot(block, dc[...], preferred_element_type=F32)
+        images[f, :, 0:K] = image[:, :K].T.astype(BF)
+        images[f, :, K : 2 * K] = image[:, K:].T.astype(BF)
 
     def window_of(s):
-        places = iota((1, FR), 1)
-        parts = []
-        for f in range(2):
-            cos, sin = cis(off_ref[0, s] * (FACET * (2 * fx + f) + places))
-            qre, qim = qre_v[...], qim_v[...]
-            ure, uim = qre * cos + qim * sin, qim * cos - qre * sin
-            if f == 1:
-                sign = jnp.where((iota((K, 1), 0) & 1) == 1, -1.0, 1.0)
-                ure, uim = ure * sign, uim * sign
-            uu[0:K] = ure.astype(BF)
-            uu[K : 2 * K] = uim.astype(BF)
-            strips = acc[FR * f : FR * (f + 1)].astype(BF)
-            mixed = jnp.dot(uu[...], strips, preferred_element_type=F32)
-            bre = mixed[:K, :K] - mixed[K:, K:]
-            bim = mixed[:K, K:] + mixed[K:, :K]
-            block = jnp.concatenate([bre, bim], 1).astype(BF)
-            image = jnp.dot(block, dc[...], preferred_element_type=F32)
-            parts += [image[:, :K].T.astype(BF), image[:, K:].T.astype(BF)]
-        window = jnp.dot(jnp.concatenate(parts, 1), dr[...], preferred_element_type=F32)
-        window = window.astype(BF)
-        for di in range(3):
-            for dj in range(4):
-                pieces[s, di * 4 + dj] = window[32 * dj : 32 * dj + 32, 128 * di : 128 * di + 128]
+        both = jnp.concatenate([images[0], images[1]], 1)
+        window = jnp.dot(both, dr[...], preferred_element_type=F32).astype(BF)
+        for k in range(12):
+            di, dj = divmod(k, 4)
+            at = halo_ks.index(k) if k in halo_ks else 11
+            pieces[s, at] = window[32 * dj : 32 * dj + 32, 128 * di : 128 * di + 128]
+
+    def finish(s, f):
+        image_of(s, f)
+        if f == 1:
+            window_of(s)
+            if s == 0:
+                pl.semaphore_wait(barrier, 33)
+            for k in range(11):
+                halo_copy(s, k).start()
+            if s >= 2:
+                sum_halo(s - 2)
 
     def sum_halo(s):
-        total = pieces[s, 1].astype(F32)
-        for k in halo_ks:
-            halo_copy(s, k).wait_recv()
+        wait_for(halo_sems.at[s], halo.at[s])
+        total = pieces[s, 11].astype(F32)
+        for k in range(11):
             total = total + halo[s, k].astype(F32)
         plane[s, own] = total.astype(BF)
-        for k in range(1, 16):
-            plane_copy(s, k, own).start()
-
-    @pl.loop(0, 64)
+        for k in range(15):
+            plane_copy(s, k).start()
+
+    @pl.loop(0, 16)
     def _(h):
-        fill(0, h, va)
-
+        for d in range(4):
+            fill(0, 4 * h + d, va)
+
+    for load in loads[:4]:
+        load.wait()
     for s in range(NSUB):
         table, after = (va, vb) if s % 2 == 0 else (vb, va)
-        strips_of(s, table, after)
-        if s == 0:
-            for load in loads[:4]:
-                load.wait()
-        window_of(s)
-        if s == 0:
-            pl.semaphore_wait(barrier, 33)
-        for k in halo_ks:
-            halo_copy(s, k).start()
-        if s >= 2:
-            sum_halo(s - 2)
+        for f in range(2):
+            if s == 0:
+                for c in range(CHUNKS // 2):
+                    sky_copy(f * CHUNKS // 2 + c).wait()
+            rows_of_facet = sky_v[FR * f : FR * f + FR, :]
+            acc[f] = jnp.dot(rows_of_facet, table[...], preferred_element_type=F32)
+            if s + 1 < NSUB:
+                for h in range(32):
+                    fill(s + 1, 32 * f + h, after)
+            if f == 1:
+                finish(s, 0)
+            elif s > 0:
+                finish(s - 1, 1)
+    finish(NSUB - 1, 1)
 
     for load in loads[4:]:
         load.wait()
@@ -283,15 +286,14 @@
     sum_halo(2)
     sum_halo(3)
     for s in range(NSUB):
-        for k in range(1, 16):
-            plane_copy(s, k, plane_peer(k, -1)[1]).wait_recv()
-    for k in range(1, 8):
-        peer = last_peer(k, 1)[0]
+        wait_for(plane_sems.at[s], plane.at[s, 0:15])
+    for k in range(7):
+        peer = last_to[k]
         outbox[k] = plane[readers_ref[peer[0] * 16 + peer[1]]]
         last_copy(k, mine).start()
     fin[mine] = plane[readers_ref[fx * 16 + fy]]
-    for k in range(1, 8):
-        last_copy(k, last_peer(k, -1)[1]).wait_recv()
+    for k in range(7):
+        last_copy(k, last_peer(k + 1, -1)[1]).wait_recv()
 
     for i in range(8):
         for j in range(16):
@@ -319,13 +321,9 @@
         for p in range(2):
             out_ref[p : p + 1, at] = jnp.sum(sums[p] * taps[:, at], axis=0, keepdims=True)
 
-    for s in range(NSUB):
-        for k in halo_ks:
-            halo_copy(s, k).wait_send()
-        for k in range(1, 16):
-            plane_copy(s, k, own).wait_send()
-    for k in range(1, 8):
-        last_copy(k, mine).wait_send()
+    wait_for(send_sems.at[0], halo)
+    wait_for(send_sems.at[1], plane.at[:, 0:15])
+    wait_for(send_sems.at[2], outbox)
 
 
 def local(sky, sub_off, readers, vis_cells, row_kernel, col_kernel):
@@ -341,14 +339,14 @@
             pltpu.VMEM((2 * FR, FACET), BF),
             pltpu.VMEM((FACET, 2 * K), BF),
             pltpu.VMEM((FACET, 2 * K), BF),
-            pltpu.VMEM((2 * FR, 2 * K), F32),
+            pltpu.VMEM((2, FR, 2 * K), F32),
             pltpu.VMEM((NSUB, 2, 64, K), F32),
             pltpu.VMEM((NSUB, 2, 64, K), F32),
-            pltpu.VMEM((2 * K, FR), BF),
+            pltpu.VMEM((2, K, 2 * K), BF),
             pltpu.VMEM((NSUB, 12, 32, 128), BF),
-            pltpu.VMEM((NSUB, 12, 32, 128), BF),
+            pltpu.VMEM((NSUB, 11, 32, 128), BF),
             pltpu.VMEM((NSUB, 16, 32, 128), BF),
-            pltpu.VMEM((8, 16, 32, 128), BF),
+            pltpu.VMEM((7, 16, 32, 128), BF),
             pltpu.VMEM((8, 16, 32, 128), BF),
             pltpu.VMEM((SUB, 2 * SUB), BF),
             pltpu.VMEM((2 * SUB, SUB), BF),
@@ -367,9 +365,10 @@
             pltpu.VMEM((8, count), F32),
             pltpu.SemaphoreType.DMA((CHUNKS,)),
             pltpu.SemaphoreType.DMA((9,)),
-            pltpu.SemaphoreType.DMA((2, NSUB, 12)),
-            pltpu.SemaphoreType.DMA((2, NSUB, 16)),
-            pltpu.SemaphoreType.DMA((2, 8)),
+            pltpu.SemaphoreType.DMA((3,)),
+            pltpu.SemaphoreType.DMA((NSUB,)),
+            pltpu.SemaphoreType.DMA((NSUB,)),
+            pltpu.SemaphoreType.DMA((7,)),
         ],
         compiler_params=pltpu.CompilerParams(
             collective_id=0, has_side_effects=True, vmem_limit_bytes=56 * 2**20

time: 54.5 us -> 52 us (0.954)
  Pallas kernels: 53 us -> 50.5 us
    pallas_call x1, Pallas kernels: 53 us -> 50.5 us  [local(): pl.pallas_call(kernel, out_shape=jax.ShapeDtypeStruct((2, count), F32), i...]
where the time goes in v3:
time: 52 us; the launch traced here: 51.9 us
  Pallas kernels  50.5 us (97%)
  local copies, waits for them, and re-layouts  1.32 us (3%)
    pallas_call x1, Pallas kernels, local(): pl.pallas_call(kernel, out_shape=jax.ShapeDtypeStruct((2, count), F32), i...  50.5 us
    unnamed x1, local copies, waits for them, and re-layouts  1.32 us

profile of v3, /device:TPU:1, one launch (start us, length us, event | category | flops | bytes accessed | tf_op | source)
XLA Modules:
  0.0 51.9 jit_solution(7483857521784863871)
XLA Ops:
  0.0 50.5 %shard_map.118 = f32[2,2048]{1,0:T(2,128)} custom-call(bf16[1024,4096]{1,0:T(8,128)(2,1)} %sky_ref.1, s32[2,4]{1,0:T(2,128)} %off_ref.1, s32[128]{0:T(128)} %readers_ref.1, s32[2,2048]{1,0:T(2,128)} %cells_ref.1, bf16[8,2048]{1,0:T(8,128)(2,1)} %rows_ref.1, f32[8,2048]{1,0:T(8,128)} %cols_ref.1, bf16[256,256]{1,0:T(8,128)(2,1)} %constant.12.clone.dc_ref, ...), custom_call_target="tpu_custom_call" | custom-call | tf_op jit(solution)/shard_map/pallas_call | solution.py:333
  50.5 1.3 %copy.14 = f32[2,2048]{1,0:T(2,128)} copy(f32[2,2048]{1,0:T(2,128)} %shard_map.118) | data formatting | bytes 32768

commit v4 on v3

--- a/solution.py
+++ b/solution.py
@@ -52,11 +52,15 @@
 
 
 def grid_tables():
-    re, im = wave(SUB, SUB, SUB)
-    et = np.stack([np.concatenate([re, im], 1), np.concatenate([-im, re], 1)])
-    et = et.reshape(2, 8, 64, 2 * SUB).transpose(1, 0, 2, 3).reshape(2 * SUB, 2 * SUB)
-    en = np.block([[re, -im], [im, re]]) / 16.0
-    return jnp.asarray(et, BF), jnp.asarray(en, BF)
+    half = SUB // 2
+    re, im = wave(SUB, half, SUB)
+    et, en = [], []
+    for r in range(2):
+        a, b = re[r::2], im[r::2]
+        rows = np.stack([np.concatenate([a.T, b.T], 1), np.concatenate([-b.T, a.T], 1)])
+        et.append(rows.reshape(2, 4, 64, SUB).transpose(1, 0, 2, 3).reshape(SUB, SUB))
+        en.append(np.block([[a, -b], [b, a]]) / 16.0)
+    return jnp.asarray(np.stack(et), BF), jnp.asarray(np.stack(en), BF)
 
 
 def cis(phase):
@@ -78,13 +82,17 @@
     return lax.broadcasted_iota(jnp.int32, shape, dim)
 
 
-def turned(kernel, start):
-    first = start & 7
-    row = iota(kernel.shape, 0)
-    laid = kernel
-    for r in range(1, 8):
-        laid = jnp.where(first == r, jnp.roll(kernel, r, 0), laid)
-    return laid, (start >> 3) + jnp.where(row < first, 1, 0)
+def turned(kernel, start, r):
+    head = (start + 1 - r) >> 1
+    first = head & 7
+    even = jnp.concatenate([kernel[e : e + 1] for e in (0, 2, 4, 6)], 0)
+    odd = jnp.concatenate([kernel[e : e + 1] for e in (1, 3, 5, 7)], 0)
+    taps = jnp.where(((start + r) & 1) == 0, even, odd)
+    taps = jnp.concatenate([taps, jnp.zeros_like(taps)], 0)
+    laid = taps
+    for turn in range(1, 8):
+        laid = jnp.where(first == turn, jnp.roll(taps, turn, 0), laid)
+    return laid, (head >> 3) + jnp.where(iota(taps.shape, 0) < first, 1, 0)
 
 
 def place_of(i, j):
@@ -96,7 +104,7 @@
 def kernel(
     sky_ref, off_ref, readers_ref, cells_ref, rows_ref, cols_ref,
     dc_ref, dr_ref, qre_ref, qim_ref, et_ref, en_ref, out_ref,
-    sky_v, va, vb, acc, coarse, fine, images, pieces, halo, plane, outbox, fin,
+    sky_v, va, vb, acc, coarse, fine, mid, images, pieces, halo, plane, outbox, fin,
     lhs, yy, grid_t, spread, taps, blocks, et, en, dc, dr, qre_v, qim_v, cells, rows, cols,
     sky_sems, load_sems, send_sems, halo_sems, plane_sems, last_sems,
 ):
@@ -199,7 +207,7 @@
         ref[at, 0:K] = (are * bre - aim * bim).astype(BF)
         ref[at, K : 2 * K] = (are * bim + aim * bre).astype(BF)
 
-    def image_of(s, f):
+    def mix(s, f):
         cos, sin = cis(off_ref[0, s] * (FACET * (2 * fx + f) + iota((1, FR), 1)))
         qre, qim = qre_v[...], qim_v[...]
         ure, uim = qre * cos + qim * sin, qim * cos - qre * sin
@@ -207,33 +215,25 @@
             sign = jnp.where((iota((K, 1), 0) & 1) == 1, -1.0, 1.0)
             ure, uim = ure * sign, uim * sign
         table = jnp.concatenate([ure, uim], 0).astype(BF)
-        strips = acc[f].astype(BF)
-        mixed = jnp.dot(table, strips, preferred_element_type=F32)
-        bre = mixed[:K, :K] - mixed[K:, K:]
-        bim = mixed[:K, K:] + mixed[K:, :K]
-        block = jnp.concatenate([bre, bim], 1).astype(BF)
-        image = jnp.dot(block, dc[...], preferred_element_type=F32)
-        images[f, :, 0:K] = image[:, :K].T.astype(BF)
-        images[f, :, K : 2 * K] = image[:, K:].T.astype(BF)
+        mixed = jnp.dot(table, acc[f].astype(BF), preferred_element_type=F32)
+        mid[f, :, 0:K] = (mixed[:K, :K] - mixed[K:, K:]).astype(BF)
+        mid[f, :, K : 2 * K] = (mixed[:K, K:] + mixed[K:, :K]).astype(BF)
+
+    def image_of(f):
+        image = jnp.dot(mid[f], dc[...], preferred_element_type=F32)
+        images[:, 2 * K * f : 2 * K * f + K] = image[:, :K].T.astype(BF)
+        images[:, 2 * K * f + K : 2 * K * f + 2 * K] = image[:, K:].T.astype(BF)
 
     def window_of(s):
-        both = jnp.concatenate([images[0], images[1]], 1)
-        window = jnp.dot(both, dr[...], preferred_element_type=F32).astype(BF)
+        window = jnp.dot(images[...], dr[...], preferred_element_type=F32).astype(BF)
         for k in range(12):
             di, dj = divmod(k, 4)
             at = halo_ks.index(k) if k in halo_ks else 11
             pieces[s, at] = window[32 * dj : 32 * dj + 32, 128 * di : 128 * di + 128]
-
-    def finish(s, f):
-        image_of(s, f)
-        if f == 1:
-            window_of(s)
-            if s == 0:
-                pl.semaphore_wait(barrier, 33)
-            for k in range(11):
-                halo_copy(s, k).start()
-            if s >= 2:
-                sum_halo(s - 2)
+        if s == 0:
+            pl.semaphore_wait(barrier, 33)
+        for k in range(11):
+            halo_copy(s, k).start()
 
     def sum_halo(s):
         wait_for(halo_sems.at[s], halo.at[s])
@@ -262,11 +262,20 @@
             if s + 1 < NSUB:
                 for h in range(32):
                     fill(s + 1, 32 * f + h, after)
-            if f == 1:
-                finish(s, 0)
-            elif s > 0:
-                finish(s - 1, 1)
-    finish(NSUB - 1, 1)
+            turn = 2 * s + f
+            if turn >= 4 and f == 0:
+                window_of(s - 2)
+            if turn >= 1:
+                mix((turn - 1) // 2, (turn - 1) % 2)
+            if turn >= 2:
+                image_of(turn % 2)
+    mix(NSUB - 1, 1)
+    window_of(NSUB - 2)
+    image_of(0)
+    image_of(1)
+    window_of(NSUB - 1)
+    sum_halo(0)
+    sum_halo(1)
 
     for load in loads[4:]:
         load.wait()
@@ -275,13 +284,14 @@
     @pl.loop(0, tiles)
     def _(t):
         at = pl.ds(pl.multiple_of(t * VTILE, VTILE), VTILE)
-        laid, block = turned(rows[:, at].astype(F32), cells[0:1, at])
-        across = iota((SUB // 8, 8, VTILE), 0)
-        weights = jnp.where(across == block[None], laid[None], 0.0)
-        spread[:, at] = weights.reshape(SUB, VTILE).astype(BF)
-        laid, block = turned(cols[:, at], cells[1:2, at])
-        taps[:, at] = laid
-        blocks[:, at] = block
+        for r in range(2):
+            laid, block = turned(rows[:, at].astype(F32), cells[0:1, at], r)
+            across = iota((SUB // 16, 8, VTILE), 0)
+            weights = jnp.where(across == block[None], laid[None], 0.0)
+            spread[256 * r : 256 * r + 256, at] = weights.reshape(SUB // 2, VTILE).astype(BF)
+            laid, block = turned(cols[:, at], cells[1:2, at], r)
+            taps[r, :, at] = laid
+            blocks[r, :, at] = block
 
     sum_halo(2)
     sum_halo(3)
@@ -295,31 +305,41 @@
     for k in range(7):
         last_copy(k, last_peer(k + 1, -1)[1]).wait_recv()
 
-    for i in range(8):
+    for i in range(4):
         for j in range(16):
-            a, b = place_of(i, j)
-            lhs[32 * j : 32 * j + 32, 128 * i : 128 * i + 128] = fin[a, b]
-    for h in range(2):
-        at = slice(SUB * h, SUB * h + SUB)
-        yy[at] = jnp.dot(lhs[...], et[:, at], preferred_element_type=F32).astype(BF)
-    for h in range(2):
-        at = slice(SUB * h, SUB * h + SUB)
-        grid_t[at] = jnp.dot(en[at], yy[...], preferred_element_type=F32).astype(BF)
+            low, high = (fin[place_of(h, j)].astype(F32) for h in (i, i + 4))
+            at = (slice(32 * j, 32 * j + 32), slice(128 * i, 128 * i + 128))
+            lhs[0, at[0], at[1]] = (low + high).astype(BF)
+            lhs[1, at[0], at[1]] = (low - high).astype(BF)
+    for r in range(2):
+        for p in range(2):
+            part = et[r, :, 256 * p : 256 * p + 256]
+            done = jnp.dot(lhs[r], part, preferred_element_type=F32)
+            low, high = done[:256], done[256:]
+            at = (slice(256 * p, 256 * p + 256), slice(256 * r, 256 * r + 256))
+            yy[0, at[0], at[1]] = (low + high).astype(BF)
+            yy[1, at[0], at[1]] = (low - high).astype(BF)
+    for r in range(2):
+        grid_t[r] = jnp.dot(en[r], yy[r], preferred_element_type=F32).astype(BF)
 
     @pl.loop(0, tiles)
     def _(t):
         at = pl.ds(pl.multiple_of(t * VTILE, VTILE), VTILE)
-        block = blocks[:, at]
-        sums = [jnp.zeros((8, VTILE), F32), jnp.zeros((8, VTILE), F32)]
-        for c in range(4):
-            here = (iota((16, 8, VTILE), 0) + 16 * c) == block[None]
+        totals = [0.0, 0.0]
+        for r in range(2):
+            block = blocks[r, :, at]
+            sums = [jnp.zeros((8, VTILE), F32), jnp.zeros((8, VTILE), F32)]
+            for c in range(2):
+                here = (iota((16, 8, VTILE), 0) + 16 * c) == block[None]
+                for p in range(2):
+                    part = grid_t[r, 256 * p + 128 * c : 256 * p + 128 * c + 128]
+                    values = jnp.dot(part, spread[:, at], preferred_element_type=F32)
+                    values = values.reshape(16, 8, VTILE)
+                    sums[p] = sums[p] + jnp.sum(jnp.where(here, values, 0.0), axis=0)
             for p in range(2):
-                part = grid_t[SUB * p + 128 * c : SUB * p + 128 * c + 128]
-                values = jnp.dot(part, spread[:, at], preferred_element_type=F32)
-                values = values.reshape(16, 8, VTILE)
-                sums[p] = sums[p] + jnp.sum(jnp.where(here, values, 0.0), axis=0)
+                totals[p] = totals[p] + sums[p] * taps[r, :, at]
         for p in range(2):
-            out_ref[p : p + 1, at] = jnp.sum(sums[p] * taps[:, at], axis=0, keepdims=True)
+            out_ref[p : p + 1, at] = jnp.sum(totals[p], axis=0, keepdims=True)
 
     wait_for(send_sems.at[0], halo)
     wait_for(send_sems.at[1], plane.at[:, 0:15])
@@ -343,19 +363,20 @@
             pltpu.VMEM((NSUB, 2, 64, K), F32),
             pltpu.VMEM((NSUB, 2, 64, K), F32),
             pltpu.VMEM((2, K, 2 * K), BF),
+            pltpu.VMEM((K, 4 * K), BF),
             pltpu.VMEM((NSUB, 12, 32, 128), BF),
             pltpu.VMEM((NSUB, 11, 32, 128), BF),
             pltpu.VMEM((NSUB, 16, 32, 128), BF),
             pltpu.VMEM((7, 16, 32, 128), BF),
             pltpu.VMEM((8, 16, 32, 128), BF),
-            pltpu.VMEM((SUB, 2 * SUB), BF),
-            pltpu.VMEM((2 * SUB, SUB), BF),
-            pltpu.VMEM((2 * SUB, SUB), BF),
+            pltpu.VMEM((2, SUB, SUB), BF),
+            pltpu.VMEM((2, SUB, SUB), BF),
+            pltpu.VMEM((2, SUB, SUB), BF),
             pltpu.VMEM((SUB, count), BF),
-            pltpu.VMEM((8, count), F32),
-            pltpu.VMEM((8, count), jnp.int32),
-            pltpu.VMEM((2 * SUB, 2 * SUB), BF),
-            pltpu.VMEM((2 * SUB, 2 * SUB), BF),
+            pltpu.VMEM((2, 8, count), F32),
+            pltpu.VMEM((2, 8, count), jnp.int32),
+            pltpu.VMEM((2, SUB, SUB), BF),
+            pltpu.VMEM((2, SUB, SUB), BF),
             pltpu.VMEM((2 * K, 2 * K), BF),
             pltpu.VMEM((4 * K, 384), BF),
             pltpu.VMEM((K, FR), F32),

time: 52 us -> 53 us (1.019)
  Pallas kernels: 50.5 us -> 51.5 us
    pallas_call x1, Pallas kernels: 50.5 us -> 51.5 us  [local(): pl.pallas_call(kernel, out_shape=jax.ShapeDtypeStruct((2, count), F32), i...]
where the time goes in v4:
time: 53 us; the launch traced here: 52.8 us
  Pallas kernels  51.5 us (97%)
  local copies, waits for them, and re-layouts  1.32 us (2%)
    pallas_call x1, Pallas kernels, local(): pl.pallas_call(kernel, out_shape=jax.ShapeDtypeStruct((2, count), F32), i...  51.5 us
    unnamed x1, local copies, waits for them, and re-layouts  1.32 us

profile of v4, /device:TPU:1, one launch (start us, length us, event | category | flops | bytes accessed | tf_op | source)
XLA Modules:
  0.0 52.8 jit_solution(3889469680359933910)
XLA Ops:
  0.0 51.5 %shard_map.118 = f32[2,2048]{1,0:T(2,128)} custom-call(bf16[1024,4096]{1,0:T(8,128)(2,1)} %sky_ref.1, s32[2,4]{1,0:T(2,128)} %off_ref.1, s32[128]{0:T(128)} %readers_ref.1, s32[2,2048]{1,0:T(2,128)} %cells_ref.1, bf16[8,2048]{1,0:T(8,128)(2,1)} %rows_ref.1, f32[8,2048]{1,0:T(8,128)} %cols_ref.1, bf16[256,256]{1,0:T(8,128)(2,1)} %constant.12.clone.dc_ref, ...), custom_call_target="tpu_custom_call" | custom-call | tf_op jit(solution)/shard_map/pallas_call | solution.py:353
  51.5 1.3 %copy.14 = f32[2,2048]{1,0:T(2,128)} copy(f32[2,2048]{1,0:T(2,128)} %shard_map.118) | data formatting | bytes 32768

commit v5 on v4

--- a/solution.py
+++ b/solution.py
@@ -126,7 +126,10 @@
     ]
     for c in range(CHUNKS):
         sky_copy(c).start()
-    for load in loads:
+        if c == CHUNKS // 2 - 1:
+            for load in loads[:4]:
+                load.start()
+    for load in loads[4:]:
         load.start()
 
     def device(x, y, z, core):
@@ -230,8 +233,8 @@
             di, dj = divmod(k, 4)
             at = halo_ks.index(k) if k in halo_ks else 11
             pieces[s, at] = window[32 * dj : 32 * dj + 32, 128 * di : 128 * di + 128]
-        if s == 0:
-            pl.semaphore_wait(barrier, 33)
+
+    def send_halo(s):
         for k in range(11):
             halo_copy(s, k).start()
 
@@ -249,14 +252,16 @@
         for d in range(4):
             fill(0, 4 * h + d, va)
 
-    for load in loads[:4]:
-        load.wait()
     for s in range(NSUB):
         table, after = (va, vb) if s % 2 == 0 else (vb, va)
         for f in range(2):
             if s == 0:
                 for c in range(CHUNKS // 2):
                     sky_copy(f * CHUNKS // 2 + c).wait()
+            if 2 * s + f == 7:
+                pl.semaphore_wait(barrier, 33)
+                for t in range(2):
+                    send_halo(t)
             rows_of_facet = sky_v[FR * f : FR * f + FR, :]
             acc[f] = jnp.dot(rows_of_facet, table[...], preferred_element_type=F32)
             if s + 1 < NSUB:
@@ -265,15 +270,20 @@
             turn = 2 * s + f
             if turn >= 4 and f == 0:
                 window_of(s - 2)
+            if turn == 1:
+                for load in loads[:4]:
+                    load.wait()
             if turn >= 1:
                 mix((turn - 1) // 2, (turn - 1) % 2)
             if turn >= 2:
                 image_of(turn % 2)
+    window_of(NSUB - 2)
+    send_halo(NSUB - 2)
     mix(NSUB - 1, 1)
-    window_of(NSUB - 2)
     image_of(0)
     image_of(1)
     window_of(NSUB - 1)
+    send_halo(NSUB - 1)
     sum_halo(0)
     sum_halo(1)
 
@@ -297,7 +307,7 @@
     sum_halo(3)
     for s in range(NSUB):
         wait_for(plane_sems.at[s], plane.at[s, 0:15])
-    for k in range(7):
+    for k in (3, 4, 1, 2, 5, 6, 0):
         peer = last_to[k]
         outbox[k] = plane[readers_ref[peer[0] * 16 + peer[1]]]
         last_copy(k, mine).start()
@@ -328,16 +338,12 @@
         totals = [0.0, 0.0]
         for r in range(2):
             block = blocks[r, :, at]
-            sums = [jnp.zeros((8, VTILE), F32), jnp.zeros((8, VTILE), F32)]
-            for c in range(2):
-                here = (iota((16, 8, VTILE), 0) + 16 * c) == block[None]
-                for p in range(2):
-                    part = grid_t[r, 256 * p + 128 * c : 256 * p + 128 * c + 128]
-                    values = jnp.dot(part, spread[:, at], preferred_element_type=F32)
-                    values = values.reshape(16, 8, VTILE)
-                    sums[p] = sums[p] + jnp.sum(jnp.where(here, values, 0.0), axis=0)
+            here = iota((SUB // 16, 8, VTILE), 0) == block[None]
+            values = jnp.dot(grid_t[r], spread[:, at], preferred_element_type=F32)
+            values = values.reshape(2, SUB // 16, 8, VTILE)
             for p in range(2):
-                totals[p] = totals[p] + sums[p] * taps[r, :, at]
+                picked = jnp.sum(jnp.where(here, values[p], 0.0), axis=0)
+                totals[p] = totals[p] + picked * taps[r, :, at]
         for p in range(2):
             out_ref[p : p + 1, at] = jnp.sum(totals[p], axis=0, keepdims=True)
 

time: 53 us -> 51.5 us (0.972)
  Pallas kernels: 51.5 us -> 50 us
    pallas_call x1, Pallas kernels: 51.5 us -> 50 us  [local(): pl.pallas_call(kernel, out_shape=jax.ShapeDtypeStruct((2, count), F32), i...]
where the time goes in v5:
time: 51.5 us; the launch traced here: 51.3 us
  Pallas kernels  50 us (97%)
  local copies, waits for them, and re-layouts  1.32 us (3%)
    pallas_call x1, Pallas kernels, local(): pl.pallas_call(kernel, out_shape=jax.ShapeDtypeStruct((2, count), F32), i...  50 us
    unnamed x1, local copies, waits for them, and re-layouts  1.32 us

profile of v5, /device:TPU:1, one launch (start us, length us, event | category | flops | bytes accessed | tf_op | source)
XLA Modules:
  0.0 51.3 jit_solution(3036211977097999338)
XLA Ops:
  0.0 50.0 %shard_map.118 = f32[2,2048]{1,0:T(2,128)} custom-call(bf16[1024,4096]{1,0:T(8,128)(2,1)} %sky_ref.1, s32[2,4]{1,0:T(2,128)} %off_ref.1, s32[128]{0:T(128)} %readers_ref.1, s32[2,2048]{1,0:T(2,128)} %cells_ref.1, bf16[8,2048]{1,0:T(8,128)(2,1)} %rows_ref.1, f32[8,2048]{1,0:T(8,128)} %cols_ref.1, bf16[256,256]{1,0:T(8,128)(2,1)} %constant.12.clone.dc_ref, ...), custom_call_target="tpu_custom_call" | custom-call | tf_op jit(solution)/shard_map/pallas_call | solution.py:359
  50.0 1.3 %copy.14 = f32[2,2048]{1,0:T(2,128)} copy(f32[2,2048]{1,0:T(2,128)} %shard_map.118) | data formatting | bytes 32768

commit v6 on v5

--- a/solution.py
+++ b/solution.py
@@ -260,8 +260,8 @@
                     sky_copy(f * CHUNKS // 2 + c).wait()
             if 2 * s + f == 7:
                 pl.semaphore_wait(barrier, 33)
-                for t in range(2):
-                    send_halo(t)
+                send_halo(0)
+                send_halo(1)
             rows_of_facet = sky_v[FR * f : FR * f + FR, :]
             acc[f] = jnp.dot(rows_of_facet, table[...], preferred_element_type=F32)
             if s + 1 < NSUB:
@@ -284,8 +284,6 @@
     image_of(1)
     window_of(NSUB - 1)
     send_halo(NSUB - 1)
-    sum_halo(0)
-    sum_halo(1)
 
     for load in loads[4:]:
         load.wait()
@@ -303,8 +301,8 @@
             taps[r, :, at] = laid
             blocks[r, :, at] = block
 
-    sum_halo(2)
-    sum_halo(3)
+    for s in range(NSUB):
+        sum_halo(s)
     for s in range(NSUB):
         wait_for(plane_sems.at[s], plane.at[s, 0:15])
     for k in (3, 4, 1, 2, 5, 6, 0):
@@ -332,7 +330,7 @@
     for r in range(2):
         grid_t[r] = jnp.dot(en[r], yy[r], preferred_element_type=F32).astype(BF)
 
-    @pl.loop(0, tiles)
+    @pl.loop(0, tiles, unroll=4)
     def _(t):
         at = pl.ds(pl.multiple_of(t * VTILE, VTILE), VTILE)
         totals = [0.0, 0.0]

time: 51.5 us -> 50.5 us (0.981)
  Pallas kernels: 50 us -> 48.9 us
    pallas_call x1, Pallas kernels: 50 us -> 48.9 us  [local(): pl.pallas_call(kernel, out_shape=jax.ShapeDtypeStruct((2, count), F32), i...]
where the time goes in v6:
time: 50.5 us; the launch traced here: 50.3 us
  Pallas kernels  48.9 us (97%)
  local copies, waits for them, and re-layouts  1.32 us (3%)
    pallas_call x1, Pallas kernels, local(): pl.pallas_call(kernel, out_shape=jax.ShapeDtypeStruct((2, count), F32), i...  48.9 us
    unnamed x1, local copies, waits for them, and re-layouts  1.32 us

profile of v6, /device:TPU:1, one launch (start us, length us, event | category | flops | bytes accessed | tf_op | source)
XLA Modules:
  0.0 50.3 jit_solution(1988278150290895510)
XLA Ops:
  0.0 48.9 %shard_map.118 = f32[2,2048]{1,0:T(2,128)} custom-call(bf16[1024,4096]{1,0:T(8,128)(2,1)} %sky_ref.1, s32[2,4]{1,0:T(2,128)} %off_ref.1, s32[128]{0:T(128)} %readers_ref.1, s32[2,2048]{1,0:T(2,128)} %cells_ref.1, bf16[8,2048]{1,0:T(8,128)(2,1)} %rows_ref.1, f32[8,2048]{1,0:T(8,128)} %cols_ref.1, bf16[256,256]{1,0:T(8,128)(2,1)} %constant.12.clone.dc_ref, ...), custom_call_target="tpu_custom_call" | custom-call | tf_op jit(solution)/shard_map/pallas_call | solution.py:357
  49.0 1.3 %copy.14 = f32[2,2048]{1,0:T(2,128)} copy(f32[2,2048]{1,0:T(2,128)} %shard_map.118) | data formatting | bytes 32768
